TPU v7x, 128 devices: a whole 4x4x4 slice. The times are simulated.
128 devices in a mesh: dp: 8 (over x, core), seq: 16 (over z, y).
Axes of the slice: x: 4, y: 4, z: 4, core: 2. Of those that a mesh axis runs over, the one named last changes fastest.
Arguments:
- tokens: bfloat16 [16, 4096, 1024], P('dp', 'seq'), may hold values from -8 to 8
- lengths: int32 [16], P('dp'), may hold values from 1 to 4096, as said below
- cotangent: bfloat16 [16, 4096, 1024], P('dp', 'seq'), may hold values from -6 to 6
- norm_gain: bfloat16 [1024], replicated, may hold values from 0.5 to 1.5
- in_weight: bfloat16 [1024, 3072], replicated, may hold values from -0.1875 to 0.1875
- gate_down: bfloat16 [1024, 16], replicated, may hold values from -0.1875 to 0.1875
- gate_up: bfloat16 [512, 16], replicated, may hold values from -1.5 to 1.5
- gate_bias: bfloat16 [512], replicated, may hold values from 0.5 to 6
- head_gain: bfloat16 [256], replicated, may hold values from 0.5 to 1.5
- out_weight: bfloat16 [1024, 1024], replicated, may hold values from -0.1875 to 0.1875
- mlp_gain: bfloat16 [1024], replicated, may hold values from 0.5 to 1.5
- up_weight: bfloat16 [1024, 5632], replicated, may hold values from -0.1875 to 0.1875
- down_weight: bfloat16 [2816, 1024], replicated, may hold values from -0.109375 to 0.109375
Outputs:
- output: bfloat16 [16, 4096, 1024], P('dp', 'seq')
- input_grad: bfloat16 [16, 4096, 1024], P('dp', 'seq')
- grad_norm_gain: float32 [1024], P('seq')
- grad_in_weight: float32 [1024, 3072], P('seq')
- grad_gate_down: float32 [1024, 16], P('seq')
- grad_gate_up: float32 [512, 16], P('seq')
- grad_gate_bias: float32 [512], P('seq')
- grad_head_gain: float32 [256], P('seq')
- grad_out_weight: float32 [1024, 1024], P('seq')
- grad_mlp_gain: float32 [1024], P('seq')
- grad_up_weight: float32 [1024, 5632], P('seq')
- grad_down_weight: float32 [2816, 1024], P('seq')
Inputs may be any that keep to these rules, and one draw needn't show every extreme that they name: Row r is live in its first lengths[r] of 4096 slots; of the 2 rows on each index of dp, one is live in all 4096.
All inputs are finite; a program needn't handle non-finite values.
Results may differ from a plain program's by a relative error of at most 0.012.
The roundings to bfloat16 on the way count: a program that leaves them out, or rounds other values in their place, can miss the bound.
Values sent between devices are 32-bit elements; how exact they have to be, the bound alone decides.
No kernel may reach another device: no remote copies, remote signals or barrier semaphores. Data moves between devices by JAX's collectives and lax.ppermute only.
A program may use at most 320 MiB of HBM per device.

v0:
```python
import functools

import jax
import jax.numpy as jnp
import numpy as np
from jax import lax
from jax.experimental import pallas as pl
from jax.experimental.pallas import tpu as pltpu
from jax.sharding import PartitionSpec as P

F32 = jnp.float32
BF16 = jnp.bfloat16
D = 1024
FF = 2816
HEADS = 4
KHEAD = 128
VHEAD = 256
KD = 512
VALUE = 1024
ROWS = 2
SEG = 256
BLK = 128
N = ROWS * SEG
SEQ = 16
TILE = 256
EPSILON = 1e-06
VMEM_LIMIT = 64 * 1024 * 1024


def params(**kw):
    return pltpu.CompilerParams(vmem_limit_bytes=VMEM_LIMIT, **kw)


def cost(us):
    return pl.CostEstimate(flops=0, bytes_accessed=int(us * 3e6), transcendentals=0)


def dot(a, b, ca=1, cb=0):
    return lax.dot_general(a, b, (((ca,), (cb,)), ((), ())), preferred_element_type=F32)


def split(a):
    high = a.astype(BF16)
    return high, (a - high.astype(F32)).astype(BF16)


def dot3(a, b, ca=1, cb=0):
    ah, al = split(a)
    bh, bl = split(b)
    return dot(ah, bh, ca, cb) + (dot(ah, bl, ca, cb) + dot(al, bh, ca, cb))


def dot_ones(ones, b, ca=1, cb=0):
    high = b.astype(BF16)
    rest = b - high.astype(F32)
    mid = rest.astype(BF16)
    low = (rest - mid.astype(F32)).astype(BF16)
    return dot(ones, high, ca, cb) + (dot(ones, mid, ca, cb) + dot(ones, low, ca, cb))


def sigmoid(u):
    return 1.0 / (1.0 + jnp.exp(-u))


def inverse_rms(u):
    return lax.rsqrt(jnp.mean(u * u, -1, keepdims=True) + EPSILON)


def live(lengths_ref, table_ref, row, first, count, width):
    where = lax.broadcasted_iota(jnp.int32, (count, width), 0) + (first + table_ref[46] * SEG)
    return (where < lengths_ref[row]).astype(F32)


def lower(shape):
    return lax.broadcasted_iota(jnp.int32, shape, 0) >= lax.broadcasted_iota(jnp.int32, shape, 1)


def proj_kernel(
    lengths_ref, table_ref, tok_ref, gain_ref, w_ref, gd_ref, gu_ref, gb_ref,
    k_ref, v_ref, normed_ref, ld_ref, cl_ref, logit_ref, low_ref, upd_ref, out_ref,
    kc_ref,
):
    n = pl.program_id(0)

    @pl.when(n == 0)
    def _():
        inputs = tok_ref[...].astype(F32)
        normed = (inputs * inverse_rms(inputs) * gain_ref[...].astype(F32)).astype(BF16)
        normed_ref[...] = normed
        low = dot(normed, gd_ref[...], 1, 1)
        low_ref[...] = low
        low_high, low_low = split(low)
        logit = dot(low_high, gu_ref[...]) + dot(low_low, gu_ref[...])
        logit = logit + gb_ref[...].astype(F32)
        logit_ref[...] = logit
        ones = lower((BLK, BLK)).astype(BF16)
        key = dot(normed, w_ref[...])
        for row in range(ROWS):
            for part in range(SEG // BLK):
                at = row * SEG + part * BLK
                here = slice(at, at + BLK)
                alive = live(lengths_ref, table_ref, row, part * BLK, BLK, KD)
                u = logit[here]
                log_gate = (jnp.minimum(u, 0.0) - jnp.log1p(jnp.exp(-jnp.abs(u)))) * (1.0 / 16.0)
                decay = dot_ones(ones, log_gate * alive)
                ld_ref[here] = decay
                m = row * (SEG // BLK) + part
                closing = decay[BLK - 1 : BLK]
                cl_ref[m : m + 1] = closing
                k_ref[here] = key[here] * alive
                kc_ref[here] = key[here] * alive * jnp.exp(closing - decay)
        cl_ref[4:8] = jnp.zeros((4, KD), F32)

    for step in (1, 2):

        @pl.when(n == step)
        def _():
            acc = dot(normed_ref[...], w_ref[...])
            for row in range(ROWS):
                values = []
                for part in range(SEG // BLK):
                    at = row * SEG + part * BLK
                    value = acc[at : at + BLK] * live(lengths_ref, table_ref, row, part * BLK, BLK, KD)
                    v_ref[at : at + BLK] = value
                    values.append(value)
                for sub in range(2):
                    head = (step - 1) * 2 + sub
                    chan = slice(head * KHEAD, (head + 1) * KHEAD)
                    total = None
                    for part in range(SEG // BLK):
                        at = row * SEG + part * BLK
                        m = row * (SEG // BLK) + part
                        update = dot3(
                            values[part][:, sub * VHEAD : (sub + 1) * VHEAD],
                            kc_ref[at : at + BLK, chan], 0, 0,
                        )
                        upd_ref[row, part, head] = update
                        if total is None:
                            total = update
                        else:
                            total = jnp.exp(cl_ref[m : m + 1, chan]) * total + update
                    base = row * (SEG // BLK)
                    gone = cl_ref[base : base + 1, chan] + cl_ref[base + 1 : base + 2, chan]
                    for half in range(2):
                        piece = (row * HEADS + head) * 2 + half
                        out_ref[piece, 0:128] = total[half * 128 : (half + 1) * 128]
                        out_ref[piece, 128:136] = jnp.broadcast_to(gone, (8, KHEAD))


def project(lengths, table, tokens, gain, w, gd, gu, gb):
    full = lambda shape: pl.BlockSpec(shape, lambda n, s, c: (0,) * len(shape))
    return pl.pallas_call(
        proj_kernel,
        grid_spec=pltpu.PrefetchScalarGridSpec(
            num_scalar_prefetch=2,
            grid=(3,),
            in_specs=[
                full((N, D)), full((1, D)), pl.BlockSpec((D, KD), lambda n, s, c: (0, n + 1)),
                full((16, D)), full((16, KD)), full((1, KD)),
            ],
            out_specs=[
                full((N, KD)), pl.BlockSpec((N, KD), lambda n, s, c: (0, jnp.maximum(n - 1, 0))),
                full((N, D)), full((N, KD)), full((8, KD)),
                full((N, KD)), full((N, 16)), full((ROWS, 2, HEADS, VHEAD, KHEAD)),
                full((SEQ, 136, KHEAD)),
            ],
            scratch_shapes=[pltpu.VMEM((N, KD), F32)],
        ),
        out_shape=[
            jax.ShapeDtypeStruct((N, KD), F32), jax.ShapeDtypeStruct((N, VALUE), F32),
            jax.ShapeDtypeStruct((N, D), BF16),
            jax.ShapeDtypeStruct((N, KD), F32), jax.ShapeDtypeStruct((8, KD), F32),
            jax.ShapeDtypeStruct((N, KD), F32), jax.ShapeDtypeStruct((N, 16), F32),
            jax.ShapeDtypeStruct((ROWS, 2, HEADS, VHEAD, KHEAD), F32),
            jax.ShapeDtypeStruct((SEQ, 136, KHEAD), F32),
        ],
        compiler_params=params(),
        cost_estimate=cost(10),
        name="project",
    )(lengths, table, tokens, gain, w, gd, gu, gb)


def rest_kernel(table_ref, normed_ref, w_ref, cot_ref, q_ref, og_ref, normt_ref, cots_ref):
    n = pl.program_id(0)
    acc = dot(normed_ref[...], w_ref[...])

    @pl.when(n == 0)
    def _():
        q_ref[...] = acc * KHEAD ** (-0.5)
        normt_ref[...] = normed_ref[...].T.astype(F32)

    @pl.when(n > 0)
    def _():
        og_ref[...] = acc

    @pl.when(n == 2)
    def _():
        cots_ref[...] = cot_ref[:, pl.ds(pl.multiple_of((1 - table_ref[40]) * 512, 512), 512)].astype(F32)


def project_rest(table, normed, w, cot):
    full = lambda shape: pl.BlockSpec(shape, lambda n, c: (0,) * len(shape))
    return pl.pallas_call(
        rest_kernel,
        grid_spec=pltpu.PrefetchScalarGridSpec(
            num_scalar_prefetch=1,
            grid=(3,),
            in_specs=[
                full((N, D)), pl.BlockSpec((D, KD), lambda n, c: (0, jnp.where(n == 0, 0, n + 3))), full((N, D)),
            ],
            out_specs=[
                full((N, KD)), pl.BlockSpec((N, KD), lambda n, c: (0, jnp.maximum(n - 1, 0))),
                full((D, N)), full((N, KD)),
            ],
        ),
        out_shape=[
            jax.ShapeDtypeStruct((N, KD), F32), jax.ShapeDtypeStruct((N, VALUE), F32),
            jax.ShapeDtypeStruct((D, N), F32), jax.ShapeDtypeStruct((N, KD), F32),
        ],
        compiler_params=params(),
        cost_estimate=cost(0.1),
        name="project_rest",
    )(table, normed, w, cot)


def local_kernel(q_ref, k_ref, v_ref, ld_ref, out_ref):
    mask = lower((BLK, BLK))
    for head in range(HEADS):
        chan = slice(head * KHEAD, (head + 1) * KHEAD)
        vals = slice(head * VHEAD, (head + 1) * VHEAD)
        decay = ld_ref[:, chan]
        centre = decay[BLK // 2 - 1 : BLK // 2]
        scores = dot3(q_ref[:, chan] * jnp.exp(decay - centre), k_ref[:, chan] * jnp.exp(centre - decay), 1, 1)
        out_ref[:, vals] = dot3(jnp.where(mask, scores, 0.0), v_ref[:, vals])


def local(q, k, v, ld):
    rows = lambda width: pl.BlockSpec((BLK, width), lambda m: (m, 0))
    return pl.pallas_call(
        local_kernel,
        grid=(4,),
        in_specs=[rows(KD), rows(KD), rows(VALUE), rows(KD)],
        out_specs=rows(VALUE),
        out_shape=jax.ShapeDtypeStruct((N, VALUE), F32),
        compiler_params=params(),
        cost_estimate=cost(0.1),
        name="local",
    )(q, k, v, ld)


def hidden_kernel(cot_ref, wd_ref, out_ref):
    out_ref[...] = dot(cot_ref[...], wd_ref[...], 1, 1)


def hidden_grad(cot, dnw):
    return pl.pallas_call(
        hidden_kernel,
        grid=(2,),
        in_specs=[pl.BlockSpec((N, D), lambda t: (0, 0)), pl.BlockSpec((FF // 2, D), lambda t: (t, 0))],
        out_specs=pl.BlockSpec((N, FF // 2), lambda t: (0, t)),
        out_shape=jax.ShapeDtypeStruct((N, FF), F32),
        compiler_params=params(),
        cost_estimate=cost(0.1),
        name="hidden_grad",
    )(cot, dnw)


def prefix_kernel(backward, part_ref, decay_ref, out_ref):
    run = jnp.zeros((128, KHEAD), F32)
    order = range(SEQ - 1, -1, -1) if backward else range(SEQ)
    for seg in order:
        out_ref[seg] = run
        run = jnp.exp(decay_ref[seg, 0:1]) * run + part_ref[seg, 0:128]


def prefix(parts, decays, backward):
    return pl.pallas_call(
        functools.partial(prefix_kernel, backward),
        grid=(1,),
        in_specs=[
            pl.BlockSpec((SEQ, 128, KHEAD), lambda n: (0, 0, 0)),
            pl.BlockSpec((SEQ, 8, KHEAD), lambda n: (0, 16, 0)),
        ],
        out_specs=pl.BlockSpec((SEQ, 128, KHEAD), lambda n: (0, 0, 0)),
        out_shape=jax.ShapeDtypeStruct((SEQ, 128, KHEAD), F32),
        compiler_params=params(),
        cost_estimate=cost(0.1),
        name="prefix",
    )(parts, decays)


def attend_kernel(
    q_ref, og_ref, ld_ref, within_ref, cl_ref, inc_ref, upd_ref, tok_ref, ow_ref, hg_ref, mg_ref,
    heads_ref, middle_ref, mlp_ref, both_ref,
    mixed_ref,
):
    m = pl.program_id(0)
    second = lax.rem(m, 2) == 1
    previous = cl_ref[pl.ds(m - lax.rem(m, 2), 1), :]
    gain = hg_ref[...].astype(F32)
    for head in range(HEADS):
        chan = slice(head * KHEAD, (head + 1) * KHEAD)
        vals = slice(head * VHEAD, (head + 1) * VHEAD)
        start = inc_ref[0, head]
        start = jnp.where(second, jnp.exp(previous[:, chan]) * start + upd_ref[0, 0, head], start)
        out = within_ref[:, vals] + dot3(q_ref[:, chan] * jnp.exp(ld_ref[:, chan]), start, 1, 1)
        heads_ref[:, vals] = out
        gate = og_ref[:, vals]
        mixed = out * inverse_rms(out) * gain * (gate * sigmoid(gate))
        mixed_ref[:, vals] = mixed.astype(BF16)

    middle = tok_ref[...].astype(F32) + dot(mixed_ref[...], ow_ref[...])
    middle_ref[...] = middle
    mlp_in = (middle * inverse_rms(middle) * mg_ref[...].astype(F32)).astype(BF16)
    mlp_ref[...] = mlp_in
    both_ref[:D] = mlp_in.T.astype(F32)
    both_ref[D:] = mixed_ref[...].T.astype(F32)


def attend(q, og, ld, within, cl, incoming, upd, tokens, ow, hg, mg):
    full = lambda shape: pl.BlockSpec(shape, lambda m: (0,) * len(shape))
    rows = lambda width: pl.BlockSpec((BLK, width), lambda m: (m, 0))
    return pl.pallas_call(
        attend_kernel,
        grid=(4,),
        in_specs=[
            rows(KD), rows(VALUE), rows(KD), rows(VALUE), full((8, KD)),
            pl.BlockSpec((1, HEADS, VHEAD, KHEAD), lambda m: (m // 2, 0, 0, 0)),
            pl.BlockSpec((1, 1, HEADS, VHEAD, KHEAD), lambda m: (m // 2, 0, 0, 0, 0)),
            rows(D), full((VALUE, D)), full((1, VHEAD)), full((1, D)),
        ],
        out_specs=[
            rows(VALUE), rows(D), rows(D), pl.BlockSpec((D + VALUE, BLK), lambda m: (0, m)),
        ],
        out_shape=[
            jax.ShapeDtypeStruct((N, VALUE), F32), jax.ShapeDtypeStruct((N, D), F32),
            jax.ShapeDtypeStruct((N, D), BF16), jax.ShapeDtypeStruct((D + VALUE, N), F32),
        ],
        scratch_shapes=[pltpu.VMEM((BLK, VALUE), BF16)],
        compiler_params=params(),
        cost_estimate=cost(13),
        name="attend",
    )(q, og, ld, within, cl, incoming, upd, tokens, ow, hg, mg)


TILES = FF // TILE


def mlp_kernel(
    core_ref, mlp_ref, dh_ref, wg_ref, wu_ref, wd_ref, middle_ref,
    out_ref, dmlp_ref, own_ref, send_ref, hidt_ref, acc_ref,
):
    t = pl.program_id(0)

    @pl.when(t == 0)
    def _():
        acc_ref[...] = middle_ref[...]
        dmlp_ref[...] = jnp.zeros((N, D), F32)

    mlp_in = mlp_ref[...]
    gate = dot(mlp_in, wg_ref[...])
    up = dot(mlp_in, wu_ref[...])
    d_hidden = dh_ref[...]
    sig = sigmoid(gate)
    act = gate * sig
    hidden = (act * up).astype(BF16)
    d_gate = (d_hidden * up * (sig * (1.0 + gate * (1.0 - sig)))).astype(BF16)
    d_up = (d_hidden * act).astype(BF16)
    acc_ref[...] += dot(hidden, wd_ref[...])
    dmlp_ref[...] += dot(d_gate, wg_ref[...], 1, 1) + dot(d_up, wu_ref[...], 1, 1)
    first = core_ref[40] == 0
    own_ref[...] = jnp.where(first, d_gate, d_up)
    send_ref[...] = jnp.where(first, d_up, d_gate).astype(F32)
    hidt_ref[...] = hidden.T.astype(F32)

    @pl.when(t == TILES - 1)
    def _():
        out_ref[...] = acc_ref[...].astype(BF16)


def mlp(core, mlp_in, d_hidden, upw, dnw, middle):
    full = lambda shape: pl.BlockSpec(shape, lambda t, c: (0,) * len(shape))
    column = lambda rows: pl.BlockSpec((rows, TILE), lambda t, c: (0, t))
    return pl.pallas_call(
        mlp_kernel,
        grid_spec=pltpu.PrefetchScalarGridSpec(
            num_scalar_prefetch=1,
            grid=(TILES,),
            in_specs=[
                full((N, D)), column(N), column(D),
                pl.BlockSpec((D, TILE), lambda t, c: (0, TILES + t)),
                pl.BlockSpec((TILE, D), lambda t, c: (t, 0)), full((N, D)),
            ],
            out_specs=[
                full((N, D)), full((N, D)), column(N), column(N),
                pl.BlockSpec((TILE, N), lambda t, c: (t, 0)),
            ],
            scratch_shapes=[pltpu.VMEM((N, D), F32)],
        ),
        out_shape=[
            jax.ShapeDtypeStruct((N, D), BF16), jax.ShapeDtypeStruct((N, D), F32),
            jax.ShapeDtypeStruct((N, FF), BF16), jax.ShapeDtypeStruct((N, FF), F32),
            jax.ShapeDtypeStruct((FF, N), F32),
        ],
        compiler_params=params(),
        cost_estimate=cost(30),
        name="mlp",
    )(core, mlp_in, d_hidden, upw, upw, dnw, middle)


def down_grad_kernel(
    table_ref, hid_ref, hid_other, cot_ref, cot_other, keep_ref, send_ref, cotb_ref, hidb_ref
):
    @pl.when(pl.program_id(0) == 0)
    def _():
        cotb_ref[:N] = cot_ref[...]
        cotb_ref[N:] = cot_other[...].astype(BF16)

    hidb_ref[:, :N] = hid_ref[...].reshape(TILE, N).astype(BF16)
    hidb_ref[:, N:] = hid_other[...].reshape(TILE, N).astype(BF16)
    down = dot(hidb_ref[...], cotb_ref[...]).reshape(SEQ, 16, 512)
    for slab in range(4):
        slot = table_ref[41 + slab]

        @pl.when(slot < 2)
        def _():
            keep_ref[slot] = down[:, :, slab * 128 : (slab + 1) * 128]

        @pl.when(slot >= 2)
        def _():
            send_ref[slot - 2] = down[:, :, slab * 128 : (slab + 1) * 128]


def down_grad(table, hid, hid_other, cot, cot_other):
    tall = pl.BlockSpec((SEQ, 16, N), lambda t, c: (0, t, 0))
    out = pl.BlockSpec((2, SEQ, 16, 128), lambda t, c: (0, 0, t, 0))
    return pl.pallas_call(
        down_grad_kernel,
        grid_spec=pltpu.PrefetchScalarGridSpec(
            num_scalar_prefetch=1,
            grid=(TILES,),
            in_specs=[
                tall, tall, pl.BlockSpec((N, 512), lambda t, c: (0, c[40])),
                pl.BlockSpec((N, 512), lambda t, c: (0, 0)),
            ],
            out_specs=[out, out],
            scratch_shapes=[pltpu.VMEM((2 * N, 512), BF16), pltpu.VMEM((TILE, 2 * N), BF16)],
        ),
        out_shape=[jax.ShapeDtypeStruct((2, SEQ, 176, 128), F32)] * 2,
        compiler_params=params(),
        cost_estimate=cost(0.1),
        name="down_grad",
    )(table, chunks(hid), chunks(hid_other), cot, cot_other)


def up_grad_kernel(
    table_ref, mlpt_ref, mlpt_other, act_ref, act_other, keep_0, send_0, keep_1, send_1,
    left_ref, right_ref, value_ref,
):
    @pl.when(pl.program_id(0) == 0)
    def _():
        left_ref[:, :N] = mlpt_ref[...].astype(BF16)
        left_ref[:, N:] = mlpt_other[...].astype(BF16)

    right_ref[:N] = act_ref[...]
    right_ref[N:] = act_other[...].astype(BF16)
    value_ref[...] = dot(left_ref[...], right_ref[...])
    for v, (keep_ref, send_ref) in enumerate(((keep_0, send_0), (keep_1, send_1))):
        cols = slice(v * 128, v * 128 + 128)
        for index in range(8):
            keep_ref[index] = value_ref[chunk_rows(table_ref, v, index), cols]
            send_ref[index] = value_ref[chunk_rows(table_ref, v, 8 + index), cols]


def chunk_rows(table_ref, v, index):
    return pl.ds(pl.multiple_of(table_ref[v * 16 + index] * 64, 64), 64)


def up_grad(table, mlpt, mlpt_other, act, act_other):
    full = lambda shape: pl.BlockSpec(shape, lambda t, c: (0,) * len(shape))
    wide = pl.BlockSpec((N, TILE), lambda t, c: (0, t))
    return pl.pallas_call(
        up_grad_kernel,
        grid_spec=pltpu.PrefetchScalarGridSpec(
            num_scalar_prefetch=1,
            grid=(TILES,),
            in_specs=[full((D, N)), full((D, N)), wide, wide],
            out_specs=[pl.BlockSpec((8, 64, 128), lambda t, c: (0, t, 0))] * 4,
            scratch_shapes=[
                pltpu.VMEM((D, 2 * N), BF16), pltpu.VMEM((2 * N, TILE), BF16), pltpu.VMEM((D, TILE), F32),
            ],
        ),
        out_shape=[jax.ShapeDtypeStruct((8, TILES * 64, 128), F32)] * 4,
        compiler_params=params(),
        cost_estimate=cost(0.1),
        name="up_grad",
    )(table, mlpt, mlpt_other, act, act_other)


def back_kernel(
    core_ref, middle_ref, dmlp_ref, cot_ref, mg_ref, ow_ref, hg_ref, heads_ref, og_ref, q_ref, ld_ref, cl_ref,
    dmid_ref, datt_ref, mgg_ref, hgg_ref, dheads_ref, dog_ref, sends_ref, adj_ref, out_ref,
    dmix_ref,
):
    away = pl.ds(pl.multiple_of((1 - core_ref[40]) * 512, 512), 512)
    m = pl.program_id(0)

    @pl.when(m == 0)
    def _():
        mgg_ref[...] = jnp.zeros((1, D), F32)
        hgg_ref[...] = jnp.zeros((1, VHEAD), F32)

    middle = middle_ref[...]
    scale_two = inverse_rms(middle)
    unit_two = middle * scale_two
    grad = dmlp_ref[...]
    mgg_ref[...] += jnp.sum(grad * unit_two, 0, keepdims=True)
    scaled = grad * mg_ref[...].astype(F32)
    d_middle = scale_two * (scaled - unit_two * jnp.mean(scaled * unit_two, -1, keepdims=True))
    d_middle = d_middle + cot_ref[...].astype(F32)
    dmid_ref[...] = d_middle
    datt_ref[...] = d_middle.astype(BF16)
    dmix_ref[...] = dot(datt_ref[...], ow_ref[...], 1, 1)
    block = m + 1 - 2 * lax.rem(m, 2)
    first = lax.rem(m, 2) == 0
    closing = cl_ref[pl.ds(block, 1), :]
    gain = hg_ref[...].astype(F32)
    for head in range(HEADS):
        chan = slice(head * KHEAD, (head + 1) * KHEAD)
        vals = slice(head * VHEAD, (head + 1) * VHEAD)
        out = heads_ref[:, vals]
        scale = inverse_rms(out)
        unit = out * scale
        gate = og_ref[:, vals]
        sig = sigmoid(gate)
        act = gate * sig
        d_mixed = dmix_ref[:, vals]
        dog_ref[:, vals] = (d_mixed * (unit * gain) * (sig * (1.0 + gate * (1.0 - sig)))).astype(BF16)
        d_norm = d_mixed * act
        hgg_ref[...] += jnp.sum(d_norm * unit, 0, keepdims=True)
        scaled = d_norm * gain
        d_out = scale * (scaled - unit * jnp.mean(scaled * unit, -1, keepdims=True))
        dheads_ref[:, vals] = d_out
        adjoint = dot3(d_out, q_ref[:, chan] * jnp.exp(ld_ref[:, chan]), 0, 0)

        @pl.when(first)
        def _():
            adj_ref[0, head] = adjoint

        @pl.when(jnp.logical_not(first))
        def _():
            total = jnp.exp(closing[:, chan]) * adj_ref[0, head] + adjoint
            for half in range(2):
                out_ref[head * 2 + half] = total[half * 128 : (half + 1) * 128]

    sends_ref[:, :512] = datt_ref[:, away].astype(F32)
    sends_ref[:, 512:] = dog_ref[:, away].astype(F32)


def back(core, middle, dmlp, cot, mg, ow, hg, heads, og, q, ld, cl):
    full = lambda shape: pl.BlockSpec(shape, lambda m, c: (0,) * len(shape))
    block = lambda m: m + 1 - 2 * lax.rem(m, 2)
    wide = pl.BlockSpec((BLK, D), lambda m, c: (block(m), 0))
    return pl.pallas_call(
        back_kernel,
        grid_spec=pltpu.PrefetchScalarGridSpec(num_scalar_prefetch=1, grid=(4,), in_specs=[
            wide, wide, wide, full((1, D)), full((VALUE, D)), full((1, VHEAD)),
            pl.BlockSpec((BLK, VALUE), lambda m, c: (block(m), 0)),
            pl.BlockSpec((BLK, VALUE), lambda m, c: (block(m), 0)),
            pl.BlockSpec((BLK, KD), lambda m, c: (block(m), 0)),
            pl.BlockSpec((BLK, KD), lambda m, c: (block(m), 0)),
            full((8, KD)),
        ],
        out_specs=[
            wide, wide, full((1, D)), full((1, VHEAD)),
            pl.BlockSpec((BLK, VALUE), lambda m, c: (block(m), 0)),
            pl.BlockSpec((BLK, VALUE), lambda m, c: (block(m), 0)),
            pl.BlockSpec((BLK, D), lambda m, c: (block(m), 0)),
            pl.BlockSpec((1, HEADS, VHEAD, KHEAD), lambda m, c: (m // 2, 0, 0, 0)),
            pl.BlockSpec((8, 128, KHEAD), lambda m, c: (m // 2, 0, 0)),
        ],
        scratch_shapes=[pltpu.VMEM((BLK, VALUE), F32)]),
        out_shape=[
            jax.ShapeDtypeStruct((N, D), F32), jax.ShapeDtypeStruct((N, D), BF16),
            jax.ShapeDtypeStruct((1, D), F32), jax.ShapeDtypeStruct((1, VHEAD), F32),
            jax.ShapeDtypeStruct((N, VALUE), F32), jax.ShapeDtypeStruct((N, VALUE), BF16),
            jax.ShapeDtypeStruct((N, D), F32),
            jax.ShapeDtypeStruct((ROWS, HEADS, VHEAD, KHEAD), F32),
            jax.ShapeDtypeStruct((SEQ, 128, KHEAD), F32),
        ],
                compiler_params=params(),
        cost_estimate=cost(30),
        name="back",
    )(core, middle, dmlp, cot, mg, ow, hg, heads, og, q, ld, cl)


def inner_kernel(
    limit_ref, core_ref, q_ref, k_ref, v_ref, dout_ref, ld_ref, cl_ref, inc_ref, ret_ref, upd_ref, adj_ref,
    logit_ref, low_ref, gu_ref, normed_ref, hg_ref, mg_ref,
    dproj_ref, dprojs_ref, dlow_ref, pack_ref,
    dlg_ref, gb_ref, gup_ref, gdn_ref,
):
    m = pl.program_id(0)
    row = m // 2
    part = lax.rem(m, 2)
    second = part == 1

    @pl.when(m == 0)
    def _():
        gb_ref[...] = jnp.zeros((1, KD), F32)
        gup_ref[...] = jnp.zeros((16, KD), F32)
        gdn_ref[...] = jnp.zeros((16, D), F32)

    mask = lower((BLK, BLK))
    upper = lax.broadcasted_iota(jnp.int32, (BLK, BLK), 0) <= lax.broadcasted_iota(jnp.int32, (BLK, BLK), 1)
    upper = upper.astype(BF16)
    closing = cl_ref[pl.ds(m, 1), :]
    previous = cl_ref[pl.ds(row * 2, 1), :]
    following = cl_ref[pl.ds(row * 2 + 1, 1), :]
    alive = live(limit_ref, core_ref, row, part * BLK, BLK, VHEAD)
    alive_key = alive[:, :KHEAD]
    for head in range(HEADS):
        chan = slice(head * KHEAD, (head + 1) * KHEAD)
        vals = slice(head * VHEAD, (head + 1) * VHEAD)
        start = inc_ref[0, head]
        start = jnp.where(second, jnp.exp(previous[:, chan]) * start + upd_ref[0, 0, head], start)
        update = jnp.where(second, upd_ref[0, 1, head], upd_ref[0, 0, head])
        end_state = jnp.exp(closing[:, chan]) * start + update
        end_grad = ret_ref[0, head]
        end_grad = jnp.where(second, end_grad, jnp.exp(following[:, chan]) * end_grad + adj_ref[0, head])
        decay = ld_ref[:, chan]
        centre = decay[BLK // 2 - 1 : BLK // 2]
        query = q_ref[:, chan]
        key = k_ref[:, chan]
        value = v_ref[:, vals]
        d_out = dout_ref[:, vals]
        up_factor = jnp.exp(decay - centre)
        down_factor = jnp.exp(centre - decay)
        query_mid = query * up_factor
        key_mid = key * down_factor
        close_factor = jnp.exp(closing[:, chan] - decay)
        scores = jnp.where(mask, dot3(query_mid, key_mid, 1, 1), 0.0)
        d_scores = jnp.where(mask, dot3(d_out, value, 1, 1), 0.0)
        d_query = up_factor * dot3(d_scores, key_mid) + jnp.exp(decay) * dot3(d_out, start)
        d_key = down_factor * dot3(d_scores, query_mid, 0, 0) + close_factor * dot3(value, end_grad)
        d_value = dot3(scores, d_out, 0, 0) + dot3(key * close_factor, end_grad, 1, 1)
        d_decay = query * d_query - key * d_key
        dlg_ref[:, chan] = dot_ones(upper, d_decay) + jnp.sum(end_grad * end_state, 0, keepdims=True)
        dproj_ref[:, chan] = (d_query * KHEAD ** (-0.5)).astype(BF16)
        dproj_ref[:, KD + head * KHEAD : KD + (head + 1) * KHEAD] = (d_key * alive_key).astype(BF16)
        dproj_ref[:, 2 * KD + head * VHEAD : 2 * KD + (head + 1) * VHEAD] = (d_value * alive).astype(BF16)
    alive_gate = live(limit_ref, core_ref, row, part * BLK, BLK, KD)
    d_logit = dlg_ref[...] * alive_gate * (1.0 / (1.0 + jnp.exp(logit_ref[...]))) * (1.0 / 16.0)
    gb_ref[...] += jnp.sum(d_logit, 0, keepdims=True)
    gup_ref[...] += dot3(low_ref[...], d_logit, 0, 0)
    high, rest = split(d_logit)
    d_low = (dot(high, gu_ref[...], 1, 1) + dot(rest, gu_ref[...], 1, 1)).astype(BF16)
    dlow_ref[...] = d_low
    gdn_ref[...] += dot(d_low, normed_ref[...], 0, 0)
    away = pl.ds(pl.multiple_of((1 - core_ref[40]) * 1024, 1024), 1024)
    dprojs_ref[...] = dproj_ref[:, away].astype(F32)

    @pl.when(m == 3)
    def _():
        pack_ref[:, 16:24] = jnp.zeros((SEQ, 8, 128), F32)
        for chunk in range(SEQ):
            pack_ref[chunk, :16, :64] = gdn_ref[:, chunk * 64 : chunk * 64 + 64]
            pack_ref[chunk, :16, 64:96] = gup_ref[:, chunk * 32 : chunk * 32 + 32]
            pack_ref[chunk, :16, 96:] = jnp.zeros((16, 32), F32)
            pack_ref[chunk, 16:17, 64:] = mg_ref[:, chunk * 64 : chunk * 64 + 64]
            pack_ref[chunk, 17:18, :32] = gb_ref[:, chunk * 32 : chunk * 32 + 32]
            pack_ref[chunk, 17:18, 32:48] = hg_ref[:, chunk * 16 : chunk * 16 + 16]


def inner(limit, core, q, k, v, dout, ld, cl, incoming, returned, upd, adj, logit, low, gu, normed, hg, mg):
    full = lambda shape: pl.BlockSpec(shape, lambda m, s, c: (0,) * len(shape))
    by_row = pl.BlockSpec((1, HEADS, VHEAD, KHEAD), lambda m, s, c: (m // 2, 0, 0, 0))
    return pl.pallas_call(
        inner_kernel,
        grid_spec=pltpu.PrefetchScalarGridSpec(
            num_scalar_prefetch=2,
            grid=(4,),
            in_specs=[
                pl.BlockSpec((BLK, KD), lambda m, s, c: (m, 0)), pl.BlockSpec((BLK, KD), lambda m, s, c: (m, 0)),
                pl.BlockSpec((BLK, VALUE), lambda m, s, c: (m, 0)), pl.BlockSpec((BLK, VALUE), lambda m, s, c: (m, 0)),
                pl.BlockSpec((BLK, KD), lambda m, s, c: (m, 0)), full((8, KD)),
                by_row, by_row,
                pl.BlockSpec((1, 2, HEADS, VHEAD, KHEAD), lambda m, s, c: (m // 2, 0, 0, 0, 0)),
                by_row,
                pl.BlockSpec((BLK, KD), lambda m, s, c: (m, 0)), pl.BlockSpec((BLK, 16), lambda m, s, c: (m, 0)),
                full((16, KD)), pl.BlockSpec((BLK, D), lambda m, s, c: (m, 0)), full((1, VHEAD)), full((1, D)),
            ],
            out_specs=[
                pl.BlockSpec((BLK, 2048), lambda m, s, c: (m, 0)),
                pl.BlockSpec((BLK, 1024), lambda m, s, c: (m, 0)), pl.BlockSpec((BLK, 16), lambda m, s, c: (m, 0)),
                full((SEQ, 24, 128)),
            ],
            scratch_shapes=[
                pltpu.VMEM((BLK, KD), F32), pltpu.VMEM((1, KD), F32), pltpu.VMEM((16, KD), F32), pltpu.VMEM((16, D), F32),
            ],
        ),
        out_shape=[
            jax.ShapeDtypeStruct((N, 2048), BF16), jax.ShapeDtypeStruct((N, 1024), F32), jax.ShapeDtypeStruct((N, 16), BF16),
            jax.ShapeDtypeStruct((SEQ, 24, 128), F32),
        ],
        compiler_params=params(),
        cost_estimate=cost(300),
        name="inner",
    )(limit, core, q, k, v, dout, ld, cl, incoming, returned, upd, adj, logit, low, gu, normed, hg, mg)


def outer_kernel(sets, extras, table_ref, *refs):
    count = 4 * len(sets)
    more, outs = refs[count : count + extras], refs[count + extras : -3]
    left_ref, right_ref, value_ref = refs[-3:]
    at = 0
    for which, streams in enumerate(sets):
        x_ref, x_other, y_ref, y_other = refs[4 * which : 4 * which + 4]
        left_ref[:, :N] = x_ref[...].astype(BF16)
        left_ref[:, N:] = x_other[...].astype(BF16)
        for part, v in enumerate(streams):
            cols = slice(part * 512, (part + 1) * 512)
            right_ref[:N] = y_ref[:, cols]
            right_ref[N:] = y_other[:, cols].astype(BF16)
            value_ref[...] = dot(left_ref[...], right_ref[...])
            for side, target in enumerate(outs[2 * at : 2 * at + 2]):
                for index in range(8):
                    rows = chunk_rows(table_ref, v, side * 8 + index)
                    for slab in range(4):
                        target[index, slab * 64 : slab * 64 + 64] = value_ref[rows, slab * 128 : slab * 128 + 128]
                    if extras:
                        own, first, got, pack = more
                        chunk = table_ref[v * 16 + side * 8 + index]
                        cut = slice(v * 88, v * 88 + 88)
                        target[index, 256:344] = own[0, chunk, cut] + first[0, chunk, cut] + got[chunk, cut]
                        if v == 1:
                            target[index, 344:368] = pack[chunk]
            at += 1


def outer(table, sets, more=()):
    operands, specs, outs = [], [], []
    for x, x_other, rows, y, y_other, cols, streams in sets:
        width = 512 * len(streams)
        operands += [x, x_other, y, y_other]
        specs += [
            pl.BlockSpec((D, N), lambda i, t, r=rows: (r, 0)), pl.BlockSpec((D, N), lambda i, t, r=rows: (r, 0)),
            pl.BlockSpec((N, width), lambda i, t: (0, t[40])), pl.BlockSpec((N, width), lambda i, t, c=cols: (0, c)),
        ]
        for v in streams:
            total = 256 + (88 + 24 * v if more else 0)
            outs += [jax.ShapeDtypeStruct((8, total, 128), F32)] * 2
    for array in more:
        operands.append(array)
        if array.ndim == 4:
            specs.append(pl.BlockSpec((1,) + array.shape[1:], lambda i, t: (t[45], 0, 0, 0)))
        else:
            specs.append(pl.BlockSpec(array.shape, lambda i, t: (0, 0, 0)))
    return pl.pallas_call(
        functools.partial(outer_kernel, [streams for *_, streams in sets], len(more)),
        grid_spec=pltpu.PrefetchScalarGridSpec(
            num_scalar_prefetch=1, grid=(1,), in_specs=specs,
            out_specs=[pl.BlockSpec(out.shape, lambda i, t: (0, 0, 0)) for out in outs],
            scratch_shapes=[
                pltpu.VMEM((D, 2 * N), BF16), pltpu.VMEM((2 * N, 512), BF16), pltpu.VMEM((D, 512), F32),
            ],
        ),
        out_shape=outs,
        compiler_params=params(),
        cost_estimate=cost(0.1),
        name="outer",
    )(table, *operands)


def input_kernel(
    y_ref, og_ref, w_ref, dlow_ref, gd_ref, tok_ref, gain_ref, dmid_ref, pack_in,
    grad_ref, pack_ref, acc_ref,
):
    t = pl.program_id(0)

    @pl.when(t == 0)
    def _():
        acc_ref[...] = dot(dlow_ref[...], gd_ref[...])

    @pl.when(t < 4)
    def _():
        acc_ref[...] += dot(y_ref[...], w_ref[...], 1, 1)

    @pl.when(t >= 4)
    def _():
        acc_ref[...] += dot(og_ref[...], w_ref[...], 1, 1)

    @pl.when(t == 5)
    def _():
        total = jnp.zeros((1, D), F32)
        for at in range(0, N, 128):
            here = slice(at, at + 128)
            inputs = tok_ref[here].astype(F32)
            scale = inverse_rms(inputs)
            unit = inputs * scale
            grad = acc_ref[here]
            total = total + jnp.sum(grad * unit, 0, keepdims=True)
            scaled = grad * gain_ref[...].astype(F32)
            d_inputs = scale * (scaled - unit * jnp.mean(scaled * unit, -1, keepdims=True))
            grad_ref[here] = (dmid_ref[here] + d_inputs).astype(BF16)
        pack_ref[...] = pack_in[...]
        for chunk in range(SEQ):
            pack_ref[chunk, 16:17, :64] = total[:, chunk * 64 : chunk * 64 + 64]


def input_back(y, og, w, dlow, gd, tokens, gain, dmid, pack):
    full = lambda shape: pl.BlockSpec(shape, lambda t: (0,) * len(shape))
    return pl.pallas_call(
        input_kernel,
        grid=(6,),
        in_specs=[
            pl.BlockSpec((N, 512), lambda t: (0, jnp.minimum(t, 3))),
            pl.BlockSpec((N, 512), lambda t: (0, jnp.maximum(t - 4, 0))),
            pl.BlockSpec((D, 512), lambda t: (0, t)),
            full((N, 16)), full((16, D)), full((N, D)), full((1, D)), full((N, D)),
            full((SEQ, 24, 128)),
        ],
        out_specs=[full((N, D)), full((SEQ, 24, 128))],
        out_shape=[
            jax.ShapeDtypeStruct((N, D), BF16), jax.ShapeDtypeStruct((SEQ, 24, 128), F32),
        ],
        scratch_shapes=[pltpu.VMEM((N, D), F32)],
        compiler_params=params(),
        cost_estimate=cost(12),
        name="input_back",
    )(y, og, w, dlow, gd, tokens, gain, dmid, pack)


SWAP = [(i, i ^ 1) for i in range(8)]
FLIP = {0: 1, 1: 3}
XORDER = ((0, 1), (1, 0))
ORDERS = (((0, 1, 2, 3), (1, 0, 3, 2)), ((2, 3, 0, 1), (3, 2, 1, 0)))


def bit_of(seq, which):
    at = seq // 4 if which < 2 else seq % 4
    return at // 2 if which % 2 else int(at in (1, 2))


def chunk_of(order, bits):
    value = dict(zip(order, bits))
    along = [[0, 1, 3, 2][2 * value[2 * a + 1] + value[2 * a]] for a in range(2)]
    return along[0] * 4 + along[1]


def partner(seq, which):
    z, y = seq // 4, seq % 4
    return (z ^ FLIP[which]) * 4 + y if which < 2 else z * 4 + (y ^ FLIP[which - 2])


def tables():
    table = np.zeros((128, 96), np.int32)
    for device in range(128):
        core, seq = (device // 16) % 2, device % 16
        for v in range(2):
            order = ORDERS[v][core]
            chunks = [chunk_of(order, [(i >> 3) & 1, (i >> 2) & 1, (i >> 1) & 1, i & 1]) for i in range(16)]
            mine = [bit_of(seq, which) for which in order]
            table[device, v * 16 : v * 16 + 8] = chunks[mine[0] * 8 : mine[0] * 8 + 8]
            table[device, v * 16 + 8 : v * 16 + 16] = chunks[(1 - mine[0]) * 8 : (1 - mine[0]) * 8 + 8]
            table[device, 32 + v * 4 : 36 + v * 4] = mine
            for slot in range(16):
                table[device, 48 + v * 16 + chunks[slot ^ (8 * mine[0])]] = slot
        table[device, 40] = core
        table[device, 46] = seq
        x, (near, far) = device // 32, XORDER[core]
        for slab in range(4):
            away = bit_of(slab * 4, near) != bit_of(x * 4, near)
            table[device, 41 + slab] = bit_of(slab * 4, far) + 2 * away
        table[device, 45] = bit_of(x * 4, far)
        for who in range(2):
            near, far = XORDER[core ^ who]
            table[device, 80 + 4 * who : 84 + 4 * who] = [x, x ^ FLIP[far], x ^ FLIP[near], x ^ 2]
    return table


TABLE = tables()
STEPS = [
    [
        [(d, (d // 16) * 16 + partner(d % 16, ORDERS[v][(d // 16) % 2][step])) for d in range(128)]
        for step in range(4)
    ]
    for v in range(2)
]
ACROSS = [
    [(i, ((i // 2) ^ FLIP[XORDER[i % 2][step]]) * 2 + i % 2) for i in range(8)] for step in range(2)
]


def exchange(value):
    return lax.all_to_all(value, "seq", 0, 0, tiled=True)


def swap(value):
    return lax.ppermute(value, "dp", SWAP)


def halve_x_kernel(table_ref, k_ref, r_ref, send_ref):
    del table_ref
    send_ref[...] = k_ref[...] + r_ref[...]


def halve_x(table, keep, got):
    rows = keep.shape[1] // 2
    theirs = pl.BlockSpec((1, rows, 128), lambda j, t: (1 - t[45], j, 0))
    return pl.pallas_call(
        halve_x_kernel,
        grid_spec=pltpu.PrefetchScalarGridSpec(
            num_scalar_prefetch=1, grid=(2,), in_specs=[theirs, theirs],
            out_specs=pl.BlockSpec((1, rows, 128), lambda j, t: (0, j, 0)),
        ),
        out_shape=jax.ShapeDtypeStruct((1, 2 * rows, 128), F32),
        compiler_params=params(),
        cost_estimate=cost(0.1),
        name="halve_x",
    )(table, keep, got)


def halve_kernel(shapes, moves, table_ref, *refs):
    del table_ref
    ins = list(refs)
    at = 0
    values = []
    for groups, later in shapes:
        row, parts = 0, []
        rests = ins[at + 2 * groups : at + 2 * groups + later]
        for group in range(groups):
            k_ref, r_ref = ins[at + 2 * group : at + 2 * group + 2]
            parts.append((row, row + k_ref.shape[1], k_ref, r_ref))
            row += k_ref.shape[1]
        values.append((parts, rests))
        at += 2 * groups + later
    for v, first, count, out, place in moves:
        out_ref = ins[at + out]
        for low, high, k_ref, r_ref in values[v][0]:
            start, stop = max(first, low), min(first + count, high)
            if start >= stop:
                continue
            total = k_ref[:, start - low : stop - low] + r_ref[:, start - low : stop - low]
            for rest in values[v][1]:
                total = total + rest[:, start:stop]
            out_ref[:, place + start - first : place + stop - first] = total


def halve(table, step, streams, moves=None):
    size = 2 if step < 3 else 1
    turns = 2 if step == 1 else 1
    operands, specs, shapes, totals = [], [], [], []
    for v, (groups, later) in enumerate(streams):
        bit = lambda t, n, v=v: t[32 + v * 4 + n]

        def block(i, t, bit=bit):
            if step == 1:
                return (1 - bit(t, 1)) * 2 + i
            if step == 2:
                return bit(t, 1) * 2 + 1 - bit(t, 2)
            last = 1 - bit(t, 3) if step == 3 else bit(t, 3)
            return bit(t, 1) * 4 + bit(t, 2) * 2 + last

        total = 0
        for pair in groups:
            for array in pair:
                operands.append(array)
                specs.append(pl.BlockSpec((size, array.shape[1], 128), lambda i, t, f=block: (f(i, t), 0, 0)))
            total += pair[0].shape[1]
        for array in later:
            operands.append(array)
            count = array.shape[0] // size
            specs.append(
                pl.BlockSpec((size, total, 128), lambda i, t, f=block, c=count: (lax.rem(f(i, t), c), 0, 0))
            )
        shapes.append((len(groups), len(later)))
        totals.append(total)
    if moves is None:
        moves = [(v, 0, totals[v], v, 0) for v in range(2)]
        outs = [(size * turns, total) for total in totals]
    else:
        outs = [(1, sum(totals))]
    return pl.pallas_call(
        functools.partial(halve_kernel, shapes, moves),
        grid_spec=pltpu.PrefetchScalarGridSpec(
            num_scalar_prefetch=1, grid=(turns,), in_specs=specs,
            out_specs=[pl.BlockSpec((size, rows, 128), lambda i, t: (i, 0, 0)) for _, rows in outs],
        ),
        out_shape=[jax.ShapeDtypeStruct((count, rows, 128), F32) for count, rows in outs],
        compiler_params=params(),
        cost_estimate=cost(0.1),
        name="halve",
    )(table, *operands)


def hop(v, step, value):
    return lax.ppermute(value, ("dp", "seq"), STEPS[v][step])


def hops(step, sends):
    return [hop(v, step, sends[v]) for v in range(2)]


def along_x(step, value):
    return lax.ppermute(value, "dp", ACROSS[step])


def after(value, *others):
    return lax.optimization_barrier((value, *others))[0]


def unpack_kernel(
    table_ref, a_ref, a_other, b_ref, b_other,
    up_ref, down_ref, out_ref, in_ref, gd_ref, gu_ref, ng_ref, mg_ref, gb_ref, hg_ref,
):
    core = table_ref[40]

    def place(own_ref, other_ref, at, rows, slabs, target, first, second):
        for slab in range(slabs):
            own = own_ref[at : at + rows]
            other = other_ref[at : at + rows]
            low = jnp.where(core == 0, own, other)
            high = jnp.where(core == 0, other, own)
            target[:, first + slab * 128 : first + (slab + 1) * 128] = low
            target[:, second + slab * 128 : second + (slab + 1) * 128] = high
            at += rows
        return at

    for v in range(2):
        for tile in range(TILES):
            column = tile * TILE + v * 128
            place(a_ref, a_other, (v * TILES + tile) * 64, 64, 1, up_ref, column, FF + column)
    at = place(b_ref, b_other, 0, 64, 4, out_ref, 0, 512)
    at = place(b_ref, b_other, at, 64, 4, in_ref, 2048, 2560)
    at = place(b_ref, b_other, at, 64, 4, in_ref, 0, 1024)
    at = place(b_ref, b_other, at, 64, 4, in_ref, 512, 1536)
    small = b_ref[at : at + 24] + b_other[at : at + 24]
    gd_ref[...] = small[:16, :64]
    gu_ref[...] = small[:16, 64:96]
    ng_ref[...] = small[16:17, :64]
    mg_ref[...] = small[16:17, 64:128]
    gb_ref[...] = small[17:18, :32]
    hg_ref[...] = small[17:18, 32:48]
    for slab in range(4):
        first = at + 24 + slab * 176
        for ref, base, place_of in ((b_ref, core * 512, 80), (b_other, (1 - core) * 512, 84)):
            cols = pl.ds(pl.multiple_of(base + table_ref[place_of + slab] * 128, 128), 128)
            down_ref[:, cols] = ref[first : first + 176]


def unpack(table, a, a_other, b, b_other):
    shapes = [
        (64, 2 * FF), (176, D), (64, D), (64, 3072), (16, 64), (16, 32), (1, 64), (1, 64), (1, 32), (1, 16),
    ]
    return pl.pallas_call(
        unpack_kernel,
        in_specs=[pl.BlockSpec(memory_space=pltpu.SMEM)] + [pl.BlockSpec(memory_space=pltpu.VMEM)] * 4,
        out_specs=[pl.BlockSpec(memory_space=pltpu.VMEM)] * len(shapes),
        out_shape=[jax.ShapeDtypeStruct(shape, F32) for shape in shapes],
        compiler_params=params(),
        cost_estimate=cost(4),
        name="unpack",
    )(table, a, a_other, b, b_other)


def chunks(value):
    return value.reshape(SEQ, value.shape[0] // SEQ, value.shape[1])


def shards(
    tokens, lengths, cotangent, norm_gain, in_weight, gate_down, gate_up, gate_bias, head_gain,
    out_weight, mlp_gain, up_weight, down_weight,
):
    device = lax.axis_index("dp") * SEQ + lax.axis_index("seq")
    table = lax.dynamic_slice(jnp.asarray(TABLE), (device, 0), (1, 96)).reshape(96)
    tok = tokens.reshape(N, D)
    cot = cotangent.reshape(N, D)
    line = lambda vector: vector.reshape(1, -1)
    flat = lambda value: value.reshape(2, -1, 128)

    down_t, up_t = gate_down.T, gate_up.T
    k, v, normed, ld, cl, logit, low, upd, pieces = project(
        lengths, table, tok, line(norm_gain), in_weight, down_t, up_t, line(gate_bias)
    )
    gathered = exchange(pieces)
    q, og, normed_t, cot_send = project_rest(table, after(normed, pieces), in_weight, cot)
    incoming = prefix(after(gathered, q), gathered, False)
    normed_other, cot_other = swap(after(normed_t, incoming)), swap(after(cot_send, incoming))
    within = local(after(q, incoming), k, v, ld)
    d_hidden = hidden_grad(after(cot, within), down_weight)
    incoming = after(exchange(incoming), d_hidden).reshape(ROWS, HEADS, VHEAD, KHEAD)
    heads, middle, mlp_in, joint = attend(
        q, og, ld, within, cl, incoming, upd, tok, out_weight, line(head_gain), line(mlp_gain)
    )
    output, dmlp, act, act_send, hidden_t = mlp(
        table, after(mlp_in, normed_other, cot_other), d_hidden, up_weight, down_weight, middle
    )
    hidden_other, act_other, joint_other = swap(hidden_t), swap(act_send), swap(joint)
    dmid, datt, g_mlp_gain, g_head_gain, dheads, dog, sends, adj, pieces_back = back(
        table, middle, dmlp, cot, line(mlp_gain), out_weight, line(head_gain), heads, og, q, ld, cl
    )
    sends_other = swap(sends)
    owned = exchange(pieces_back)
    dn_keep, dn_send = down_grad(table, after(hidden_t, pieces_back), hidden_other, cot, cot_other)
    dn_got = along_x(0, after(flat(dn_send), owned))
    owned = prefix(after(owned, dn_keep), gathered, True)
    returned = exchange(owned)
    up_0, up_send_0, up_1, up_send_1 = up_grad(
        table, after(joint, owned, sends_other), joint_other, act, act_other
    )
    up_gots = hops(0, (after(up_send_0, returned), after(up_send_1, returned)))
    keep_o, send_o, keep_g, send_g = outer(
        after(table, up_0),
        [
            (joint, joint_other, 1, datt, sends_other, 0, (0,)),
            (normed_t, normed_other, 0, dog, sends_other, 1, (1,)),
        ],
    )
    four_got = hops(0, (send_o, send_g))
    dn_first = dn_got
    dn_send = halve_x(table, after(flat(dn_keep), keep_o), dn_first)
    dn_got = along_x(1, dn_send)
    returned = after(returned, dn_send).reshape(ROWS, HEADS, VHEAD, KHEAD)
    dproj, dproj_send, dlow, pack = inner(
        lengths, table, q, k, v, dheads, ld, cl, incoming, returned, upd, adj, logit, low, up_t, normed,
        g_head_gain, g_mlp_gain,
    )
    input_grad, pack = input_back(
        dproj, dog, in_weight, dlow, down_t, tok, line(norm_gain), dmid, pack
    )
    dproj_got = swap(after(dproj_send, dn_got, pack, *up_gots, *four_got))
    up = [([(after(up_0, pack), up_gots[0])], []), ([(up_1, up_gots[1])], [])]
    up_sends = halve(table, 1, up)
    up_gots = hops(1, up_sends)
    keep_p, send_p, keep_r, send_r = outer(
        after(table, up_sends[0]),
        [(normed_t, normed_other, 0, dproj, dproj_got, 0, (0, 1))],
        (dn_keep, dn_first.reshape(dn_keep.shape), dn_got.reshape(SEQ, 176, 128), pack),
    )
    first = hops(0, (send_p, send_r))
    add = lambda streams, gots: [(groups, later + [got]) for (groups, later), got in zip(streams, gots)]
    up = add([([(after(up_0, keep_p), up[0][0][0][1])], []), up[1]], up_gots)
    up_sends = halve(table, 2, up)
    up_gots = hops(2, up_sends)
    rest = [
        ([(after(keep_o, up_sends[0]), four_got[0]), (keep_p, first[0])], []),
        ([(keep_g, four_got[1]), (keep_r, first[1])], []),
    ]
    sends = halve(table, 1, rest)
    gots = hops(1, sends)
    up = add(up, up_gots)
    up_sends = halve(after(table, sends[0]), 3, up)
    up_gots = hops(3, up_sends)
    rest = add(rest, gots)
    sends = halve(after(table, up_sends[0]), 2, rest)
    gots = hops(2, sends)
    (early,) = halve(table, 4, add(up, up_gots), [(0, 0, 704, 0, 0), (1, 0, 704, 0, 704)])
    early = early[0]
    early = early + along_x(0, early)
    rest = add(rest, gots)
    sends = halve(after(table, early), 3, rest)
    gots = hops(3, sends)
    early = early + along_x(1, early)
    (late,) = halve(
        table, 4, add(rest, gots),
        [
            (0, 0, 256, 0, 0), (1, 0, 256, 0, 256), (0, 256, 256, 0, 512), (1, 256, 256, 0, 768),
            (1, 600, 24, 0, 1024), (0, 512, 88, 0, 1048), (1, 512, 88, 0, 1136),
        ],
    )
    late = late[0]
    got = along_x(1, late)
    early_other = swap(early)
    late = jnp.concatenate([late[:1048] + got[:1048], late[1048:], got[1048:]], 0)
    got = along_x(0, late)
    late = jnp.concatenate([late[:1048] + got[:1048], late[1048:], got[1048:]], 0)
    grad_up, grad_down, grad_out, grad_in, g_down, g_upf, g_norm, g_mlp, g_bias, g_head = unpack(
        table, early, early_other, late, swap(late)
    )
    return (
        output.reshape(ROWS, SEG, D),
        input_grad.reshape(ROWS, SEG, D),
        g_norm.reshape(64),
        grad_in,
        g_down.T,
        g_upf.T,
        g_bias.reshape(32),
        g_head.reshape(16),
        grad_out,
        g_mlp.reshape(64),
        grad_up,
        grad_down,
    )


def solution(mesh):
    rows = P("dp", "seq", None)
    return jax.shard_map(
        shards,
        mesh=mesh,
        in_specs=(rows, P("dp"), rows) + (P(),) * 10,
        out_specs=(
            rows, rows, P("seq"), P("seq", None), P("seq", None), P("seq", None), P("seq"), P("seq"),
            P("seq", None), P("seq"), P("seq", None), P("seq", None),
        ),
        check_vma=False,
    )
```

profile of v0, /device:TPU:1, one launch (start us, length us, event | category | flops | bytes accessed | tf_op | source)
XLA Modules:
  0.0 360.5 jit_solution(1293135668474118510)
XLA Ops:
  0.6 1.3 reshape.94.gain_ref
  1.9 1.3 reshape.95.gb_ref
  3.2 1.3 dynamic-slice_bitcast_fusion.table_ref.core_ref
  4.5 10.9 %project.1 = (f32[512,512]{1,0:T(8,128)}, f32[512,1024]{1,0:T(8,128)}, bf16[512,1024]{1,0:T(8,128)(2,1)}, f32[512,512]{1,0:T(8,128)}, f32[8,512]{1,0:T(8,128)}, ...) custom-call(s32[2]{0:T(128)} %limit_ref.1, ...), custom_call_target="tpu_custom_call" | custom-call | bytes 30000000 | tf_op jit(solution)/shard_map/project/pallas_call | solution.py:152
  15.4 8.6 %all-to-all-start = ((f32[16,136,128]{2,1,0:T(8,128)}), f32[16,136,128]{2,1,0:T(8,128)}, u32[]{:S(2)}, u32[]{:S(2)}) async-start(f32[16,136,128]{2,1,0:T(8,128)} %get-tuple-element.111), calls=%async_computation | async-start | bytes 2228224 | tf_op jit(solution)/shard_map/all_to_all | solution.py:896
  24.0 8.2 %project_rest.1 = (f32[512,512]{1,0:T(8,128)}, f32[512,1024]{1,0:T(8,128)}, f32[1024,512]{1,0:T(8,128)}, f32[512,512]{1,0:T(8,128)}) custom-call(s32[96]{0:T(128)} %dynamic-slice_bitcast_fusion.table_ref.core_ref, bf16[512,1024]{1,0:T(8,128)(2,1)} %get-tuple-element.112.normed_ref, bf16[1024,3072]{1,0:T(8,128)(2,1)} %w_ref.5, bf16[512,1024]{1,0:T(8,128)(2,1)} %bitcast.31), custom_call_target="tpu_custom_call" | custom-call | bytes 300000 | tf_op jit(solution)/shard_map/project_rest/pallas_call | solution.py:203
  32.2 8.6 %all-to-all-done.part_ref.decay_ref = f32[16,136,128]{2,1,0:T(8,128)} async-done(((f32[16,136,128]{2,1,0:T(8,128)}), f32[16,136,128]{2,1,0:T(8,128)}, u32[]{:S(2)}, u32[]{:S(2)}) %all-to-all-start) | async-done | bytes 1114144 | tf_op jit(solution)/shard_map/all_to_all | solution.py:896
  40.7 2.3 prefix.2
  43.0 2.7 collective-permute-start
  45.8 4.4 %all-to-all-start.1 = ((f32[16,128,128]{2,1,0:T(8,128)}), f32[16,128,128]{2,1,0:T(8,128)}, u32[]{:S(2)}, u32[]{:S(2)}) async-start(f32[16,128,128]{2,1,0:T(8,128)} %prefix.2), calls=%async_computation.1 | async-start | bytes 2097152 | tf_op jit(solution)/shard_map/all_to_all | solution.py:896
  51.4 7.6 %local.1.within_ref = f32[512,1024]{1,0:T(8,128)} custom-call(f32[512,512]{1,0:T(8,128)} %get-tuple-element.117.q_ref, f32[512,512]{1,0:T(8,128)} %get-tuple-element.118.k_ref, f32[512,1024]{1,0:T(8,128)} %get-tuple-element.119.v_ref, f32[512,512]{1,0:T(8,128)} %get-tuple-element.115.ld_ref), custom_call_target="tpu_custom_call" | custom-call | bytes 300000 | tf_op jit(solution)/shard_map/local/pallas_call | solution.py:239
  58.9 7.4 %hidden_grad.1.dh_ref = f32[512,2816]{1,0:T(8,128)} custom-call(bf16[512,1024]{1,0:T(8,128)(2,1)} %bitcast.32, bf16[2816,1024]{1,0:T(8,128)(2,1)} %wd_ref.3), custom_call_target="tpu_custom_call" | custom-call | bytes 300000 | tf_op jit(solution)/shard_map/hidden_grad/pallas_call | solution.py:256
  67.0 10.1 %attend.1 = (f32[512,1024]{1,0:T(8,128)}, f32[512,1024]{1,0:T(8,128)}, bf16[512,1024]{1,0:T(8,128)(2,1)}, f32[2048,512]{1,0:T(8,128)}) custom-call(f32[512,512]{1,0:T(8,128)} %get-tuple-element.117.q_ref, f32[512,1024]{1,0:T(8,128)} %get-tuple-element.114.og_ref, f32[512,512]{1,0:T(8,128)} %get-tuple-element.115.ld_ref, f32[512,1024]{1,0:T(8,128)} %local.1.within_ref, ...), custom_call_target="tpu_custom_call" | custom-call | bytes 39000000 | tf_op jit(solution)/shard_map/attend/pallas_call | solution.py:323
  77.1 26.7 %mlp.1 = (bf16[512,1024]{1,0:T(8,128)(2,1)}, f32[512,1024]{1,0:T(8,128)}, bf16[512,2816]{1,0:T(8,128)(2,1)}, f32[512,2816]{1,0:T(8,128)}, f32[2816,512]{1,0:T(8,128)}) custom-call(s32[96]{0:T(128)} %dynamic-slice_bitcast_fusion.table_ref.core_ref, bf16[512,1024]{1,0:T(8,128)(2,1)} %get-tuple-element.129.mlp_ref, f32[512,2816]{1,0:T(8,128)} %hidden_grad.1.dh_ref, ...), custom_call_target="tpu_custom_call" | custom-call | bytes 90000000 | tf_op jit(solution)/shard_map/mlp/pallas_call | solution.py:384
  103.9 1.9 collective-permute-start.2
  106.2 16.1 %back.1 = (f32[512,1024]{1,0:T(8,128)}, bf16[512,1024]{1,0:T(8,128)(2,1)}, f32[1,1024]{1,0:T(1,128)}, f32[1,256]{1,0:T(1,128)}, f32[512,1024]{1,0:T(8,128)}, /*i...) custom-call(s32[96]{0:T(128)} %dynamic-slice_bitcast_fusion.table_ref.core_r, ...), custom_call_target="tpu_custom_call" | custom-call | bytes 90000000 | tf_op jit(solution)/shard_map/back/pallas_call | solution.py:564
  122.3 4.8 %all-to-all-start.2 = ((f32[16,128,128]{2,1,0:T(8,128)}), f32[16,128,128]{2,1,0:T(8,128)}, u32[]{:S(2)}, u32[]{:S(2)}) async-start(f32[16,128,128]{2,1,0:T(8,128)} %get-tuple-element.135), calls=%async_computation.2 | async-start | bytes 2097152 | tf_op jit(solution)/shard_map/all_to_all | solution.py:896
  127.7 13.6 %down_grad.1 = (f32[2,16,176,128]{3,2,1,0:T(8,128)}, f32[2,16,176,128]{3,2,1,0:T(8,128)}) custom-call(s32[96]{0:T(128)} %dynamic-slice_bitcast_fusion.table_ref.core_ref, f32[16,176,512]{2,1,0:T(8,128)} %bitcast.39, f32[16,176,512]{2,1,0:T(8,128)} %bitcast.8.hid_other, bf16[512,1024]{1,0:T(8,128)(2,1)} %bitcast.34, f32[512,512]{1,0:T(8,128)} %collective-permute-done.1.cot_other), custom_call_target="tpu_custom_call" | custom-call | bytes 300000 | tf_op jit(solution)/shard_map/down_grad/pallas_call | solution.py:437
  141.3 2.3 all-to-all-done.2.part_ref
  143.6 2.5 collective-permute-start.6
  146.1 2.3 prefix.3
  148.4 4.7 %all-to-all-start.3 = ((f32[16,128,128]{2,1,0:T(8,128)}), f32[16,128,128]{2,1,0:T(8,128)}, u32[]{:S(2)}, u32[]{:S(2)}) async-start(f32[16,128,128]{2,1,0:T(8,128)} %prefix.3), calls=%async_computation.3 | async-start | bytes 2097152 | tf_op jit(solution)/shard_map/all_to_all | solution.py:896
  153.1 16.8 %up_grad.1 = (f32[8,704,128]{2,1,0:T(8,128)}, f32[8,704,128]{2,1,0:T(8,128)}, f32[8,704,128]{2,1,0:T(8,128)}, f32[8,704,128]{2,1,0:T(8,128)}) custom-call(s32[96]{0:T(128)} %dynamic-slice_bitcast_fusion.table_ref.core_ref, f32[2048,512]{1,0:T(8,128)} %get-tuple-element.142.mlpt_ref.refs_0_, f32[2048,512]{1,0:T(8,128)} %collective-permute-done.4.mlpt_other.refs_1_, ...), custom_call_target="tpu_custom_call" | custom-call | bytes 300000 | tf_op jit(solution)/shard_map/up_grad/pallas_call | solution.py:482
  169.9 2.6 collective-permute-start.7
  172.5 2.4 collective-permute-start.8
  174.9 8.7 %outer.2 = (f32[8,256,128]{2,1,0:T(8,128)}, f32[8,256,128]{2,1,0:T(8,128)}, f32[8,256,128]{2,1,0:T(8,128)}, f32[8,256,128]{2,1,0:T(8,128)}) custom-call(s32[96]{0:T(128)} %dynamic-slice_bitcast_fusion.table_ref.core_ref, f32[2048,512]{1,0:T(8,128)} %get-tuple-element.142.mlpt_ref.refs_0_, f32[2048,512]{1,0:T(8,128)} %collective-permute-done.4.mlpt_other.refs_1_, ...), custom_call_target="tpu_custom_call" | custom-call | bytes 300000 | tf_op jit(solution)/shard_map/outer/pallas_call | solution.py:759
  183.6 3.4 halve_x.1
  187.5 18.5 %inner.1 = (bf16[512,2048]{1,0:T(8,128)(2,1)}, f32[512,1024]{1,0:T(8,128)}, bf16[512,16]{1,0:T(8,128)(2,1)}, f32[16,24,128]{2,1,0:T(8,128)}) custom-call(s32[2]{0:T(128)} %limit_ref.1, s32[96]{0:T(128)} %dynamic-slice_bitcast_fusion.table_ref.core_ref, f32[512,512]{1,0:T(8,128)} %get-tuple-element.117.q_ref, f32[512,512]{1,0:T(8,128)} %get-tuple-element.118.k_ref, ...), custom_call_target="tpu_custom_call" | custom-call | bytes 900000000 | tf_op jit(solution)/shard_map/inner/pallas_call | solution.py:678
  206.1 11.2 %input_back.1 = (bf16[512,1024]{1,0:T(8,128)(2,1)}, f32[16,24,128]{2,1,0:T(8,128)}) custom-call(bf16[512,2048]{1,0:T(8,128)(2,1)} %get-tuple-element.159.y_ref.refs_2_, bf16[512,1024]{1,0:T(8,128)(2,1)} %get-tuple-element.148.refs_6_.og_ref, bf16[1024,3072]{1,0:T(8,128)(2,1)} %w_ref.5, bf16[512,16]{1,0:T(8,128)(2,1)} %get-tuple-element.160.dlow_ref, ...), custom_call_target="tpu_custom_call" | custom-call | bytes 36000000 | tf_op jit(solution)/shard_map/input_back/pallas_call | solution.py:813
  217.3 1.2 collective-permute-done.11.refs_5_.refs_6_.refs_7_.refs_8_
  218.7 4.6 %halve.8 = (f32[4,704,128]{2,1,0:T(8,128)}, f32[4,704,128]{2,1,0:T(8,128)}) custom-call(s32[96]{0:T(128)} %dynamic-slice_bitcast_fusion.table_ref.core_ref, f32[8,704,128]{2,1,0:T(8,128)} %get-tuple-element.178.refs_0_, f32[8,704,128]{2,1,0:T(8,128)} %collective-permute-done.7.refs_1_, f32[8,704,128]{2,1,0:T(8,128)} %get-tuple-element.168.refs_2_.refs_3_.refs_4_.refs_5_, ...), custom_call_target="tpu_custom_call" | custom-call | bytes 300000 | tf_op jit(solution)/shard_map/halve/pallas_call | solution.py:984
  223.3 1.5 collective-permute-start.13
  224.8 1.2 collective-permute-start.14
  226.0 9.9 %outer.3 = (f32[8,344,128]{2,1,0:T(8,128)}, f32[8,344,128]{2,1,0:T(8,128)}, f32[8,368,128]{2,1,0:T(8,128)}, f32[8,368,128]{2,1,0:T(8,128)}) custom-call(s32[96]{0:T(128)} %dynamic-slice_bitcast_fusion.table_ref.core_ref, f32[1024,512]{1,0:T(8,128)} %get-tuple-element.126.refs_4_.refs_0_, f32[1024,512]{1,0:T(8,128)} %collective-permute-done.refs_5_.refs_1_, ...), custom_call_target="tpu_custom_call" | custom-call | bytes 300000 | tf_op jit(solution)/shard_map/outer/pallas_call | solution.py:759
  235.9 1.8 collective-permute-start.17
  237.7 1.8 collective-permute-start.16
  239.5 2.3 collective-permute-done.13.refs_2_
  241.8 2.4 collective-permute-done.14.refs_5_.refs_6_.refs_7_
  244.2 4.1 %halve.9 = (f32[2,704,128]{2,1,0:T(8,128)}, f32[2,704,128]{2,1,0:T(8,128)}) custom-call(s32[96]{0:T(128)} %dynamic-slice_bitcast_fusion.table_ref.core_ref, f32[8,704,128]{2,1,0:T(8,128)} %get-tuple-element.178.refs_0_, f32[8,704,128]{2,1,0:T(8,128)} %collective-permute-done.7.refs_1_, f32[4,704,128]{2,1,0:T(8,128)} %collective-permute-done.13.refs_2_, ...), custom_call_target="tpu_custom_call" | custom-call | bytes 300000 | tf_op jit(solution)/shard_map/halve/pallas_call | solution.py:984
  248.2 4.4 %collective-permute-start.15 = (f32[2,704,128]{2,1,0:T(8,128)}, f32[2,704,128]{2,1,0:T(8,128)}, u32[]{:S(2)}, u32[]{:S(2)}) collective-permute-start(f32[2,704,128]{2,1,0:T(8,128)} %get-tuple-element.180), channel_id=1, source_target_pairs={{0,1},{1,0},{2,3},{3,2},{4,5},{5,4},{6,7},{7,6},{8,9},{9,8},{10,11... | collective-permute-start | bytes 2162696 | tf_op jit(solution)/shard_map/ppermute | solution.py:998
  252.6 3.3 collective-permute-start.18
  255.9 2.8 collective-permute-done.16.refs_3_
  258.7 3.7 %collective-permute-done.17.refs_7_.refs_8_.refs_9_.refs_10_ = f32[8,368,128]{2,1,0:T(8,128)} collective-permute-done((f32[8,368,128]{2,1,0:T(8,128)}, f32[8,368,128]{2,1,0:T(8,128)}, u32[]{:S(2)}, u32[]{:S(2)}) %collective-permute-start.17) | collective-permute-done | bytes 1507360 | tf_op jit(solution)/shard_map/ppermute | solution.py:998
  262.4 4.3 %halve.10 = (f32[4,600,128]{2,1,0:T(8,128)}, f32[4,624,128]{2,1,0:T(8,128)}) custom-call(s32[96]{0:T(128)} %dynamic-slice_bitcast_fusion.table_ref.core_ref, f32[8,256,128]{2,1,0:T(8,128)} %get-tuple-element.181.refs_0_, f32[8,256,128]{2,1,0:T(8,128)} %collective-permute-done.10.refs_1_, f32[8,344,128]{2,1,0:T(8,128)} %get-tuple-element.177.refs_2_, ...), custom_call_target="tpu_custom_call" | custom-call | bytes 300000 | tf_op jit(solution)/shard_map/halve/pallas_call | solution.py:984
  266.9 5.0 %collective-permute-done.15.refs_3_ = f32[2,704,128]{2,1,0:T(8,128)} collective-permute-done((f32[2,704,128]{2,1,0:T(8,128)}, f32[2,704,128]{2,1,0:T(8,128)}, u32[]{:S(2)}, u32[]{:S(2)}) %collective-permute-start.15) | collective-permute-done | bytes 720928 | tf_op jit(solution)/shard_map/ppermute | solution.py:998
  271.9 3.3 halve.11
  275.3 11.9 %collective-permute-done.19.refs_4_ = f32[1,704,128]{2,1,0:T(8,128)} collective-permute-done((f32[1,704,128]{2,1,0:T(8,128)}, f32[1,704,128]{2,1,0:T(8,128)}, u32[]{:S(2)}, u32[]{:S(2)}) %collective-permute-start.19) | collective-permute-done | bytes 360480 | tf_op jit(solution)/shard_map/ppermute | solution.py:998
  287.2 3.6 %halve.12 = f32[1,1408,128]{2,1,0:T(8,128)} custom-call(s32[96]{0:T(128)} %dynamic-slice_bitcast_fusion.table_ref.core_ref, f32[8,704,128]{2,1,0:T(8,128)} %get-tuple-element.178.refs_0_, f32[8,704,128]{2,1,0:T(8,128)} %collective-permute-done.7.refs_1_, f32[4,704,128]{2,1,0:T(8,128)} %collective-permute-done.13.refs_2_, ...), custom_call_target="tpu_custom_call" | custom-call | bytes 300000 | tf_op jit(solution)/shard_map/halve/pallas_call | solution.py:984
  291.7 3.8 %halve.13 = (f32[2,600,128]{2,1,0:T(8,128)}, f32[2,624,128]{2,1,0:T(8,128)}) custom-call(s32[96]{0:T(128)} %dynamic-slice_bitcast_fusion.table_ref.core_ref, f32[8,256,128]{2,1,0:T(8,128)} %get-tuple-element.181.refs_0_, f32[8,256,128]{2,1,0:T(8,128)} %collective-permute-done.10.refs_1_, f32[8,344,128]{2,1,0:T(8,128)} %get-tuple-element.177.refs_2_, ...), custom_call_target="tpu_custom_call" | custom-call | bytes 300000 | tf_op jit(solution)/shard_map/halve/pallas_call | solution.py:984
  296.5 2.2 collective-permute-start.26
  298.6 3.9 %collective-permute-done.21 = f32[1408,128]{1,0:T(8,128)} collective-permute-done((f32[1408,128]{1,0:T(8,128)}, f32[1408,128]{1,0:T(8,128)}, u32[]{:S(2)}, u32[]{:S(2)}) %collective-permute-start.21) | collective-permute-done | bytes 720928 | tf_op jit(solution)/shard_map/ppermute | solution.py:1006
  302.5 2.3 bitcast_add_fusion
  304.8 2.2 collective-permute-done.26.refs_5_
  307.0 3.2 halve.14
  310.6 6.0 %collective-permute-done.28.refs_6_ = f32[1,600,128]{2,1,0:T(8,128)} collective-permute-done((f32[1,600,128]{2,1,0:T(8,128)}, f32[1,600,128]{2,1,0:T(8,128)}, u32[]{:S(2)}, u32[]{:S(2)}) %collective-permute-start.28) | collective-permute-done | bytes 307232 | tf_op jit(solution)/shard_map/ppermute | solution.py:998
  316.7 3.5 halve.15
  321.2 8.7 %collective-permute-done.30 = f32[1224,128]{1,0:T(8,128)S(1)} collective-permute-done((f32[1224,128]{1,0:T(8,128)}, f32[1224,128]{1,0:T(8,128)S(1)}, u32[]{:S(2)}, u32[]{:S(2)}) %collective-permute-start.30) | collective-permute-done | bytes 626720 | tf_op jit(solution)/shard_map/ppermute | solution.py:1006
  329.8 1.1 slice_add_fusion.1
  331.0 1.3 collective-permute-start.31
  332.3 11.3 %collective-permute-done.31 = f32[1400,128]{1,0:T(8,128)S(1)} collective-permute-done((f32[1400,128]{1,0:T(8,128)S(1)}, f32[1400,128]{1,0:T(8,128)S(1)}, u32[]{:S(2)}, u32[]{:S(2)}) %collective-permute-start.31) | collective-permute-done | bytes 716832 | tf_op jit(solution)/shard_map/ppermute | solution.py:1006
  344.7 7.2 %collective-permute-start.32 = (f32[1752,128]{1,0:T(8,128)S(1)}, f32[1752,128]{1,0:T(8,128)}, u32[]{:S(2)}, u32[]{:S(2)}) collective-permute-start(f32[1752,128]{1,0:T(8,128)S(1)} %pad_maximum_fusion.b_ref), channel_id=1, source_target_pairs={{0,16},{16,0},{32,48},{48,32},{64,80},{80,64},{96,112},{112,96},{1... | collective-permute-start | bytes 2691080 | tf_op jit(solution)/shard_map/ppermute | solution.py:900
  352.9 1.0 collective-permute-start.23
  353.9 1.8 collective-permute-done.23.a_other
  356.6 3.7 %unpack.1 = (f32[64,5632]{1,0:T(8,128)}, f32[176,1024]{1,0:T(8,128)}, f32[64,1024]{1,0:T(8,128)}, f32[64,3072]{1,0:T(8,128)}, f32[16,64]{1,0:T(8,128)}, /*index=...) custom-call(s32[96]{0:T(128)} %dynamic-slice_bitcast_fusion.table_ref.core_ref, ...), custom_call_target="tpu_custom_call" | custom-call | bytes 12000000 | tf_op jit(solution)/shard_map/unpack/pallas_call | solution.py:1056
  (61 shorter events, 10.2 us)
Async XLA Ops:
  15.4 25.4 %all-to-all-start = ((f32[16,136,128]{2,1,0:T(8,128)}), f32[16,136,128]{2,1,0:T(8,128)}, u32[]{:S(2)}, u32[]{:S(2)}) async-start(f32[16,136,128]{2,1,0:T(8,128)} %get-tuple-element.111), calls=%async_computation | async-start | bytes 2228224 | tf_op jit(solution)/shard_map/all_to_all | solution.py:896
  43.0 7.2 %copy-start.5 = (bf16[256]{0:T(256)(128)(2,1)S(1)}, bf16[256]{0:T(256)(128)(2,1)}, u32[]{:S(2)}) copy-start(bf16[256]{0:T(256)(128)(2,1)} %param.22) | copy-start | bytes 1540
  43.0 7.7 %copy-start.4 = (bf16[1024]{0:T(1024)(128)(2,1)S(1)}, bf16[1024]{0:T(1024)(128)(2,1)}, u32[]{:S(2)}) copy-start(bf16[1024]{0:T(1024)(128)(2,1)} %param.24) | copy-start | bytes 6148
  43.0 34.1 %collective-permute-start = (f32[1024,512]{1,0:T(8,128)}, f32[1024,512]{1,0:T(8,128)}, u32[]{:S(2)}, u32[]{:S(2)}) collective-permute-start(f32[1024,512]{1,0:T(8,128)} %get-tuple-element.126.refs_4_.refs_0_), channel_id=1, source_target_pairs={{0,16},{16,0},{32,48},{48,32},{64,80},{80,64},{96,112},{112,96},{1... | collective-permute-start | bytes 6291464 | tf_op jit(solution)/shard_map/ppermute | solution.py:900
  45.7 31.4 %collective-permute-start.1 = (f32[512,512]{1,0:T(8,128)}, f32[512,512]{1,0:T(8,128)}, u32[]{:S(2)}, u32[]{:S(2)}) collective-permute-start(f32[512,512]{1,0:T(8,128)} %get-tuple-element.128), channel_id=1, source_target_pairs={{0,16},{16,0},{32,48},{48,32},{64,80},{80,64},{96,112},{112,96},{1... | collective-permute-start | bytes 3145736 | tf_op jit(solution)/shard_map/ppermute | solution.py:900
  45.8 21.1 %all-to-all-start.1 = ((f32[16,128,128]{2,1,0:T(8,128)}), f32[16,128,128]{2,1,0:T(8,128)}, u32[]{:S(2)}, u32[]{:S(2)}) async-start(f32[16,128,128]{2,1,0:T(8,128)} %prefix.2), calls=%async_computation.1 | async-start | bytes 2097152 | tf_op jit(solution)/shard_map/all_to_all | solution.py:896
  103.9 23.9 %collective-permute-start.2 = (f32[2816,512]{1,0:T(8,128)}, f32[2816,512]{1,0:T(8,128)}, u32[]{:S(2)}, u32[]{:S(2)}) collective-permute-start(f32[2816,512]{1,0:T(8,128)} %get-tuple-element.137), channel_id=1, source_target_pairs={{0,16},{16,0},{32,48},{48,32},{64,80},{80,64},{96,112},{112,96},{1... | collective-permute-start | bytes 17301512 | tf_op jit(solution)/shard_map/ppermute | solution.py:900
  105.7 47.4 %collective-permute-start.5 = (f32[512,2816]{1,0:T(8,128)}, f32[512,2816]{1,0:T(8,128)}, u32[]{:S(2)}, u32[]{:S(2)}) collective-permute-start(f32[512,2816]{1,0:T(8,128)} %get-tuple-element.144), channel_id=1, source_target_pairs={{0,16},{16,0},{32,48},{48,32},{64,80},{80,64},{96,112},{112,96},{1... | collective-permute-start | bytes 17301512 | tf_op jit(solution)/shard_map/ppermute | solution.py:900
  106.0 47.1 %collective-permute-start.4 = (f32[2048,512]{1,0:T(8,128)}, f32[2048,512]{1,0:T(8,128)}, u32[]{:S(2)}, u32[]{:S(2)}) collective-permute-start(f32[2048,512]{1,0:T(8,128)} %get-tuple-element.142.mlpt_ref.refs_0_), channel_id=1, source_target_pairs={{0,16},{16,0},{32,48},{48,32},{64,80},{80,64},{96,112},{112,96},{1... | collective-permute-start | bytes 12582920 | tf_op jit(solution)/shard_map/ppermute | solution.py:900
  122.3 21.3 %all-to-all-start.2 = ((f32[16,128,128]{2,1,0:T(8,128)}), f32[16,128,128]{2,1,0:T(8,128)}, u32[]{:S(2)}, u32[]{:S(2)}) async-start(f32[16,128,128]{2,1,0:T(8,128)} %get-tuple-element.135), calls=%async_computation.2 | async-start | bytes 2097152 | tf_op jit(solution)/shard_map/all_to_all | solution.py:896
  127.1 26.0 %collective-permute-start.3 = (f32[512,1024]{1,0:T(8,128)}, f32[512,1024]{1,0:T(8,128)}, u32[]{:S(2)}, u32[]{:S(2)}) collective-permute-start(f32[512,1024]{1,0:T(8,128)} %get-tuple-element.141), channel_id=1, source_target_pairs={{0,16},{16,0},{32,48},{48,32},{64,80},{80,64},{96,112},{112,96},{1... | collective-permute-start | bytes 6291464 | tf_op jit(solution)/shard_map/ppermute | solution.py:900
  143.6 40.0 %collective-permute-start.6 = (f32[2,2816,128]{2,1,0:T(8,128)}, f32[2,2816,128]{2,1,0:T(8,128)}, u32[]{:S(2)}, u32[]{:S(2)}) collective-permute-start(f32[2,2816,128]{2,1,0:T(8,128)} %bitcast.46), channel_id=1, source_target_pairs={{0,32},{16,112},{32,0},{48,80},{64,96},{80,48},{96,64},{112,16},{1... | collective-permute-start | bytes 8650760 | tf_op jit(solution)/shard_map/ppermute | solution.py:1006
  148.4 21.5 %all-to-all-start.3 = ((f32[16,128,128]{2,1,0:T(8,128)}), f32[16,128,128]{2,1,0:T(8,128)}, u32[]{:S(2)}, u32[]{:S(2)}) async-start(f32[16,128,128]{2,1,0:T(8,128)} %prefix.3), calls=%async_computation.3 | async-start | bytes 2097152 | tf_op jit(solution)/shard_map/all_to_all | solution.py:896
  169.9 48.7 %collective-permute-start.7 = (f32[8,704,128]{2,1,0:T(8,128)}, f32[8,704,128]{2,1,0:T(8,128)}, u32[]{:S(2)}, u32[]{:S(2)}) collective-permute-start(f32[8,704,128]{2,1,0:T(8,128)} %get-tuple-element.167), channel_id=1, source_target_pairs={{0,4},{1,5},{2,6},{3,7},{4,0},{5,1},{6,2},{7,3},{8,12},{9,13},{10,... | collective-permute-start | bytes 8650760 | tf_op jit(solution)/shard_map/ppermute | solution.py:998
  172.5 46.1 %collective-permute-start.8 = (f32[8,704,128]{2,1,0:T(8,128)}, f32[8,704,128]{2,1,0:T(8,128)}, u32[]{:S(2)}, u32[]{:S(2)}) collective-permute-start(f32[8,704,128]{2,1,0:T(8,128)} %get-tuple-element.170), channel_id=1, source_target_pairs={{0,1},{1,0},{2,3},{3,2},{4,5},{5,4},{6,7},{7,6},{8,9},{9,8},{10,11... | collective-permute-start | bytes 8650760 | tf_op jit(solution)/shard_map/ppermute | solution.py:998
  186.9 31.6 %collective-permute-start.9 = (f32[1,2816,128]{2,1,0:T(8,128)}, f32[1,2816,128]{2,1,0:T(8,128)}, u32[]{:S(2)}, u32[]{:S(2)}) collective-permute-start(f32[1,2816,128]{2,1,0:T(8,128)} %halve_x.1), channel_id=1, source_target_pairs={{0,96},{16,48},{32,64},{48,16},{64,32},{80,112},{96,0},{112,80},{1... | collective-permute-start | bytes 4325384 | tf_op jit(solution)/shard_map/ppermute | solution.py:1006
  186.9 30.4 %collective-permute-start.10 = (f32[8,256,128]{2,1,0:T(8,128)}, f32[8,256,128]{2,1,0:T(8,128)}, u32[]{:S(2)}, u32[]{:S(2)}) collective-permute-start(f32[8,256,128]{2,1,0:T(8,128)} %get-tuple-element.174), channel_id=1, source_target_pairs={{0,4},{1,5},{2,6},{3,7},{4,0},{5,1},{6,2},{7,3},{8,12},{9,13},{10,... | collective-permute-start | bytes 3145736 | tf_op jit(solution)/shard_map/ppermute | solution.py:998
  187.2 31.3 %collective-permute-start.11 = (f32[8,256,128]{2,1,0:T(8,128)}, f32[8,256,128]{2,1,0:T(8,128)}, u32[]{:S(2)}, u32[]{:S(2)}) collective-permute-start(f32[8,256,128]{2,1,0:T(8,128)} %get-tuple-element.175), channel_id=1, source_target_pairs={{0,1},{1,0},{2,3},{3,2},{4,5},{5,4},{6,7},{7,6},{8,9},{9,8},{10,11... | collective-permute-start | bytes 3145736 | tf_op jit(solution)/shard_map/ppermute | solution.py:998
  218.5 7.4 %collective-permute-start.12 = (f32[512,1024]{1,0:T(8,128)}, f32[512,1024]{1,0:T(8,128)}, u32[]{:S(2)}, u32[]{:S(2)}) collective-permute-start(f32[512,1024]{1,0:T(8,128)} %get-tuple-element.176), channel_id=1, source_target_pairs={{0,16},{16,0},{32,48},{48,32},{64,80},{80,64},{96,112},{112,96},{1... | collective-permute-start | bytes 6291464 | tf_op jit(solution)/shard_map/ppermute | solution.py:900
  223.3 18.5 %collective-permute-start.13 = (f32[4,704,128]{2,1,0:T(8,128)}, f32[4,704,128]{2,1,0:T(8,128)}, u32[]{:S(2)}, u32[]{:S(2)}) collective-permute-start(f32[4,704,128]{2,1,0:T(8,128)} %get-tuple-element.171), channel_id=1, source_target_pairs={{0,12},{1,13},{2,14},{3,15},{4,8},{5,9},{6,10},{7,11},{8,4},{9,5},... | collective-permute-start | bytes 4325384 | tf_op jit(solution)/shard_map/ppermute | solution.py:998
  224.8 19.4 %collective-permute-start.14 = (f32[4,704,128]{2,1,0:T(8,128)}, f32[4,704,128]{2,1,0:T(8,128)}, u32[]{:S(2)}, u32[]{:S(2)}) collective-permute-start(f32[4,704,128]{2,1,0:T(8,128)} %get-tuple-element.179), channel_id=1, source_target_pairs={{0,3},{1,2},{2,1},{3,0},{4,7},{5,6},{6,5},{7,4},{8,11},{9,10},{10,... | collective-permute-start | bytes 4325384 | tf_op jit(solution)/shard_map/ppermute | solution.py:998
  235.9 26.5 %collective-permute-start.17 = (f32[8,368,128]{2,1,0:T(8,128)}, f32[8,368,128]{2,1,0:T(8,128)}, u32[]{:S(2)}, u32[]{:S(2)}) collective-permute-start(f32[8,368,128]{2,1,0:T(8,128)} %get-tuple-element.185), channel_id=1, source_target_pairs={{0,1},{1,0},{2,3},{3,2},{4,5},{5,4},{6,7},{7,6},{8,9},{9,8},{10,11... | collective-permute-start | bytes 4521992 | tf_op jit(solution)/shard_map/ppermute | solution.py:998
  237.7 21.0 %collective-permute-start.16 = (f32[8,344,128]{2,1,0:T(8,128)}, f32[8,344,128]{2,1,0:T(8,128)}, u32[]{:S(2)}, u32[]{:S(2)}) collective-permute-start(f32[8,344,128]{2,1,0:T(8,128)} %get-tuple-element.182), channel_id=1, source_target_pairs={{0,4},{1,5},{2,6},{3,7},{4,0},{5,1},{6,2},{7,3},{8,12},{9,13},{10,... | collective-permute-start | bytes 4227080 | tf_op jit(solution)/shard_map/ppermute | solution.py:998
  248.2 23.7 %collective-permute-start.15 = (f32[2,704,128]{2,1,0:T(8,128)}, f32[2,704,128]{2,1,0:T(8,128)}, u32[]{:S(2)}, u32[]{:S(2)}) collective-permute-start(f32[2,704,128]{2,1,0:T(8,128)} %get-tuple-element.180), channel_id=1, source_target_pairs={{0,1},{1,0},{2,3},{3,2},{4,5},{5,4},{6,7},{7,6},{8,9},{9,8},{10,11... | collective-permute-start | bytes 2162696 | tf_op jit(solution)/shard_map/ppermute | solution.py:998
  252.6 19.3 %collective-permute-start.18 = (f32[2,704,128]{2,1,0:T(8,128)}, f32[2,704,128]{2,1,0:T(8,128)}, u32[]{:S(2)}, u32[]{:S(2)}) collective-permute-start(f32[2,704,128]{2,1,0:T(8,128)} %get-tuple-element.188), channel_id=1, source_target_pairs={{0,4},{1,5},{2,6},{3,7},{4,0},{5,1},{6,2},{7,3},{8,12},{9,13},{10,... | collective-permute-start | bytes 2162696 | tf_op jit(solution)/shard_map/ppermute | solution.py:998
  266.6 25.1 %collective-permute-start.25 = (f32[4,624,128]{2,1,0:T(8,128)}, f32[4,624,128]{2,1,0:T(8,128)}, u32[]{:S(2)}, u32[]{:S(2)}) collective-permute-start(f32[4,624,128]{2,1,0:T(8,128)} %get-tuple-element.192), channel_id=1, source_target_pairs={{0,3},{1,2},{2,1},{3,0},{4,7},{5,6},{6,5},{7,4},{8,11},{9,10},{10,... | collective-permute-start | bytes 3833864 | tf_op jit(solution)/shard_map/ppermute | solution.py:998
  266.9 24.8 %collective-permute-start.24 = (f32[4,600,128]{2,1,0:T(8,128)}, f32[4,600,128]{2,1,0:T(8,128)}, u32[]{:S(2)}, u32[]{:S(2)}) collective-permute-start(f32[4,600,128]{2,1,0:T(8,128)} %get-tuple-element.186), channel_id=1, source_target_pairs={{0,12},{1,13},{2,14},{3,15},{4,8},{5,9},{6,10},{7,11},{8,4},{9,5},... | collective-permute-start | bytes 3686408 | tf_op jit(solution)/shard_map/ppermute | solution.py:998
  275.2 12.0 %collective-permute-start.19 = (f32[1,704,128]{2,1,0:T(8,128)}, f32[1,704,128]{2,1,0:T(8,128)}, u32[]{:S(2)}, u32[]{:S(2)}) collective-permute-start(f32[1,704,128]{2,1,0:T(8,128)} %get-tuple-element.189), channel_id=1, source_target_pairs={{0,3},{1,2},{2,1},{3,0},{4,7},{5,6},{6,5},{7,4},{8,11},{9,10},{10,... | collective-permute-start | bytes 1081352 | tf_op jit(solution)/shard_map/ppermute | solution.py:998
  275.3 12.0 %collective-permute-start.20 = (f32[1,704,128]{2,1,0:T(8,128)}, f32[1,704,128]{2,1,0:T(8,128)}, u32[]{:S(2)}, u32[]{:S(2)}) collective-permute-start(f32[1,704,128]{2,1,0:T(8,128)} %get-tuple-element.190), channel_id=1, source_target_pairs={{0,12},{1,13},{2,14},{3,15},{4,8},{5,9},{6,10},{7,11},{8,4},{9,5},... | collective-permute-start | bytes 1081352 | tf_op jit(solution)/shard_map/ppermute | solution.py:998
  290.9 11.7 %collective-permute-start.21 = (f32[1408,128]{1,0:T(8,128)}, f32[1408,128]{1,0:T(8,128)}, u32[]{:S(2)}, u32[]{:S(2)}) collective-permute-start(f32[1408,128]{1,0:T(8,128)} %bitcast.40), channel_id=1, source_target_pairs={{0,32},{16,112},{32,0},{48,80},{64,96},{80,48},{96,64},{112,16},{1... | collective-permute-start | bytes 2162696 | tf_op jit(solution)/shard_map/ppermute | solution.py:1006
  295.5 11.4 %collective-permute-start.27 = (f32[2,624,128]{2,1,0:T(8,128)}, f32[2,624,128]{2,1,0:T(8,128)}, u32[]{:S(2)}, u32[]{:S(2)}) collective-permute-start(f32[2,624,128]{2,1,0:T(8,128)} %get-tuple-element.195), channel_id=1, source_target_pairs={{0,4},{1,5},{2,6},{3,7},{4,0},{5,1},{6,2},{7,3},{8,12},{9,13},{10,... | collective-permute-start | bytes 1916936 | tf_op jit(solution)/shard_map/ppermute | solution.py:998
  296.5 10.5 %collective-permute-start.26 = (f32[2,600,128]{2,1,0:T(8,128)}, f32[2,600,128]{2,1,0:T(8,128)}, u32[]{:S(2)}, u32[]{:S(2)}) collective-permute-start(f32[2,600,128]{2,1,0:T(8,128)} %get-tuple-element.193), channel_id=1, source_target_pairs={{0,1},{1,0},{2,3},{3,2},{4,5},{5,4},{6,7},{7,6},{8,9},{9,8},{10,11... | collective-permute-start | bytes 1843208 | tf_op jit(solution)/shard_map/ppermute | solution.py:998
  310.2 6.4 %collective-permute-start.29 = (f32[1,624,128]{2,1,0:T(8,128)}, f32[1,624,128]{2,1,0:T(8,128)}, u32[]{:S(2)}, u32[]{:S(2)}) collective-permute-start(f32[1,624,128]{2,1,0:T(8,128)} %get-tuple-element.197), channel_id=1, source_target_pairs={{0,12},{1,13},{2,14},{3,15},{4,8},{5,9},{6,10},{7,11},{8,4},{9,5},... | collective-permute-start | bytes 958472 | tf_op jit(solution)/shard_map/ppermute | solution.py:998
  310.2 6.4 %collective-permute-start.28 = (f32[1,600,128]{2,1,0:T(8,128)}, f32[1,600,128]{2,1,0:T(8,128)}, u32[]{:S(2)}, u32[]{:S(2)}) collective-permute-start(f32[1,600,128]{2,1,0:T(8,128)} %get-tuple-element.196), channel_id=1, source_target_pairs={{0,3},{1,2},{2,1},{3,0},{4,7},{5,6},{6,5},{7,4},{8,11},{9,10},{10,... | collective-permute-start | bytes 921608 | tf_op jit(solution)/shard_map/ppermute | solution.py:998
  320.2 12.1 %copy-start.1 = (f32[1408,128]{1,0:T(8,128)S(1)}, f32[1408,128]{1,0:T(8,128)}, u32[]{:S(2)}) copy-start(f32[1408,128]{1,0:T(8,128)} %bitcast_add_fusion) | copy-start | bytes 2162692
  320.2 9.6 %collective-permute-start.30 = (f32[1224,128]{1,0:T(8,128)}, f32[1224,128]{1,0:T(8,128)S(1)}, u32[]{:S(2)}, u32[]{:S(2)}) collective-permute-start(f32[1224,128]{1,0:T(8,128)} %bitcast.41), channel_id=1, source_target_pairs={{0,96},{16,48},{32,64},{48,16},{64,32},{80,112},{96,0},{112,80},{1... | collective-permute-start | bytes 1880072 | tf_op jit(solution)/shard_map/ppermute | solution.py:1006
  331.0 12.6 %collective-permute-start.31 = (f32[1400,128]{1,0:T(8,128)S(1)}, f32[1400,128]{1,0:T(8,128)S(1)}, u32[]{:S(2)}, u32[]{:S(2)}) collective-permute-start(f32[1400,128]{1,0:T(8,128)S(1)} %pad_maximum_fusion.1), channel_id=1, source_target_pairs={{0,32},{16,112},{32,0},{48,80},{64,96},{80,48},{96,64},{112,16},{1... | collective-permute-start | bytes 2150408 | tf_op jit(solution)/shard_map/ppermute | solution.py:1006
  332.3 19.6 %collective-permute-start.22 = (f32[1408,128]{1,0:T(8,128)S(1)}, f32[1408,128]{1,0:T(8,128)S(1)}, u32[]{:S(2)}, u32[]{:S(2)}) collective-permute-start(f32[1408,128]{1,0:T(8,128)S(1)} %copy-done.1), channel_id=1, source_target_pairs={{0,96},{16,48},{32,64},{48,16},{64,32},{80,112},{96,0},{112,80},{1... | collective-permute-start | bytes 2162696 | tf_op jit(solution)/shard_map/ppermute | solution.py:1006
  343.8 1.0 copy-start
  344.7 11.8 %collective-permute-start.32 = (f32[1752,128]{1,0:T(8,128)S(1)}, f32[1752,128]{1,0:T(8,128)}, u32[]{:S(2)}, u32[]{:S(2)}) collective-permute-start(f32[1752,128]{1,0:T(8,128)S(1)} %pad_maximum_fusion.b_ref), channel_id=1, source_target_pairs={{0,16},{16,0},{32,48},{48,32},{64,80},{80,64},{96,112},{112,96},{1... | collective-permute-start | bytes 2691080 | tf_op jit(solution)/shard_map/ppermute | solution.py:900
  352.0 0.9 copy-start.2
  352.9 2.8 collective-permute-start.23
  355.7 0.9 copy-start.3
where the time goes:
time: 363 us; the launch traced here: 360 us
  Pallas kernels  208 us (57%)
  waiting for transfers between devices  74.9 us (21%)
  starting transfers between devices  64.5 us (18%)
  local copies, waits for them, and re-layouts  8.65 us (2%)
    ppermute x18, waiting for transfers between devices, hop(): return lax.ppermute(value, ('dp', 'seq'), STEPS[v][step])  37.6 us
    pallas_call x8, Pallas kernels, halve(): pl.pallas_call(functools.partial(halve_kernel, shapes, moves), grid_spec=...  30.5 us
    pallas_call x1, Pallas kernels, mlp(): pl.pallas_call(mlp_kernel, grid_spec=pltpu.PrefetchScalarGridSpec(num_sca...  26.7 us
    ppermute x6, waiting for transfers between devices, along_x(): return lax.ppermute(value, 'dp', ACROSS[step])  23.9 us
    ppermute x18, starting transfers between devices, hop(): return lax.ppermute(value, ('dp', 'seq'), STEPS[v][step])  23.2 us
    all_to_all x4, starting transfers between devices, exchange(): return lax.all_to_all(value, 'seq', 0, 0, tiled=True)  22.4 us
    pallas_call x2, Pallas kernels, outer(): pl.pallas_call(functools.partial(outer_kernel, [streams for *_, streams i...  18.6 us
    pallas_call x1, Pallas kernels, inner(): pl.pallas_call(inner_kernel, grid_spec=pltpu.PrefetchScalarGridSpec(num_s...  18.5 us
  transfers between devices with their start and end apart: 37, of which 17 were waited for; matrix products, arithmetic and copies ran while one was open for 1% of the time, Pallas kernels for 44%

commit v1 on v0

--- a/solution.py
+++ b/solution.py
@@ -1163,7 +1163,7 @@
     gots = hops(3, sends)
     early = early + along_x(1, early)
     (late,) = halve(
-        table, 4, add(rest, gots),
+        after(table, early), 4, add(rest, gots),
         [
             (0, 0, 256, 0, 0), (1, 0, 256, 0, 256), (0, 256, 256, 0, 512), (1, 256, 256, 0, 768),
             (1, 600, 24, 0, 1024), (0, 512, 88, 0, 1048), (1, 512, 88, 0, 1136),

time: 363 us -> 361 us (level)
    ppermute x18, waiting for transfers between devices: 37.6 us -> 33.9 us  [hop(): return lax.ppermute(value, ('dp', 'seq'), STEPS[v][step])]
  transfers between devices with their start and end apart: 37 -> 37, of which waited for: 17 -> 19; matrix products, arithmetic and copies ran while one was open for 1% -> 2% of each run, Pallas kernels for 44% -> 45%
where the time goes in v1:
time: 361 us; the launch traced here: 358 us
  Pallas kernels  208 us (58%)
  waiting for transfers between devices  74 us (20%)
  starting transfers between devices  61.8 us (17%)
  local copies, waits for them, and re-layouts  7.73 us (2%)
  other arithmetic  5.79 us (2%)
    ppermute x18, waiting for transfers between devices, hop(): return lax.ppermute(value, ('dp', 'seq'), STEPS[v][step])  33.9 us
    pallas_call x8, Pallas kernels, halve(): pl.pallas_call(functools.partial(halve_kernel, shapes, moves), grid_spec=...  30.5 us
    pallas_call x1, Pallas kernels, mlp(): pl.pallas_call(mlp_kernel, grid_spec=pltpu.PrefetchScalarGridSpec(num_sca...  26.7 us
    ppermute x6, waiting for transfers between devices, along_x(): return lax.ppermute(value, 'dp', ACROSS[step])  25.5 us
    ppermute x18, starting transfers between devices, hop(): return lax.ppermute(value, ('dp', 'seq'), STEPS[v][step])  22.9 us
    all_to_all x4, starting transfers between devices, exchange(): return lax.all_to_all(value, 'seq', 0, 0, tiled=True)  22.4 us
    pallas_call x2, Pallas kernels, outer(): pl.pallas_call(functools.partial(outer_kernel, [streams for *_, streams i...  18.6 us
    pallas_call x1, Pallas kernels, inner(): pl.pallas_call(inner_kernel, grid_spec=pltpu.PrefetchScalarGridSpec(num_s...  18.5 us
  transfers between devices with their start and end apart: 37, of which 19 were waited for; matrix products, arithmetic and copies ran while one was open for 2% of the time, Pallas kernels for 45%

profile of v1, /device:TPU:1, one launch (start us, length us, event | category | flops | bytes accessed | tf_op | source)
XLA Modules:
  0.0 358.2 jit_solution(4068138869343435159)
XLA Ops:
  0.6 1.3 reshape.94.gain_ref
  1.9 1.3 reshape.95.gb_ref
  3.2 1.3 dynamic-slice_bitcast_fusion.table_ref.core_ref
  4.5 10.9 %project.1 = (f32[512,512]{1,0:T(8,128)}, f32[512,1024]{1,0:T(8,128)}, bf16[512,1024]{1,0:T(8,128)(2,1)}, f32[512,512]{1,0:T(8,128)}, f32[8,512]{1,0:T(8,128)}, ...) custom-call(s32[2]{0:T(128)} %limit_ref.1, ...), custom_call_target="tpu_custom_call" | custom-call | bytes 30000000 | tf_op jit(solution)/shard_map/project/pallas_call | solution.py:152
  15.3 8.7 %all-to-all-start = ((f32[16,136,128]{2,1,0:T(8,128)}), f32[16,136,128]{2,1,0:T(8,128)}, u32[]{:S(2)}, u32[]{:S(2)}) async-start(f32[16,136,128]{2,1,0:T(8,128)} %get-tuple-element.112), calls=%async_computation | async-start | bytes 2228224 | tf_op jit(solution)/shard_map/all_to_all | solution.py:896
  24.0 8.2 %project_rest.1 = (f32[512,512]{1,0:T(8,128)}, f32[512,1024]{1,0:T(8,128)}, f32[1024,512]{1,0:T(8,128)}, f32[512,512]{1,0:T(8,128)}) custom-call(s32[96]{0:T(128)} %dynamic-slice_bitcast_fusion.table_ref.core_ref, bf16[512,1024]{1,0:T(8,128)(2,1)} %get-tuple-element.113.normed_ref, bf16[1024,3072]{1,0:T(8,128)(2,1)} %w_ref.5, bf16[512,1024]{1,0:T(8,128)(2,1)} %bitcast.31), custom_call_target="tpu_custom_call" | custom-call | bytes 300000 | tf_op jit(solution)/shard_map/project_rest/pallas_call | solution.py:203
  32.2 8.6 %all-to-all-done.part_ref.decay_ref = f32[16,136,128]{2,1,0:T(8,128)} async-done(((f32[16,136,128]{2,1,0:T(8,128)}), f32[16,136,128]{2,1,0:T(8,128)}, u32[]{:S(2)}, u32[]{:S(2)}) %all-to-all-start) | async-done | bytes 1114144 | tf_op jit(solution)/shard_map/all_to_all | solution.py:896
  40.8 2.3 prefix.2
  43.0 2.7 collective-permute-start
  45.8 4.3 %all-to-all-start.1 = ((f32[16,128,128]{2,1,0:T(8,128)}), f32[16,128,128]{2,1,0:T(8,128)}, u32[]{:S(2)}, u32[]{:S(2)}) async-start(f32[16,128,128]{2,1,0:T(8,128)} %prefix.2), calls=%async_computation.1 | async-start | bytes 2097152 | tf_op jit(solution)/shard_map/all_to_all | solution.py:896
  51.3 7.6 %local.1.within_ref = f32[512,1024]{1,0:T(8,128)} custom-call(f32[512,512]{1,0:T(8,128)} %get-tuple-element.118.q_ref, f32[512,512]{1,0:T(8,128)} %get-tuple-element.119.k_ref, f32[512,1024]{1,0:T(8,128)} %get-tuple-element.120.v_ref, f32[512,512]{1,0:T(8,128)} %get-tuple-element.116.ld_ref), custom_call_target="tpu_custom_call" | custom-call | bytes 300000 | tf_op jit(solution)/shard_map/local/pallas_call | solution.py:239
  58.9 7.4 %hidden_grad.1.dh_ref = f32[512,2816]{1,0:T(8,128)} custom-call(bf16[512,1024]{1,0:T(8,128)(2,1)} %bitcast.32, bf16[2816,1024]{1,0:T(8,128)(2,1)} %wd_ref.3), custom_call_target="tpu_custom_call" | custom-call | bytes 300000 | tf_op jit(solution)/shard_map/hidden_grad/pallas_call | solution.py:256
  67.0 10.1 %attend.1 = (f32[512,1024]{1,0:T(8,128)}, f32[512,1024]{1,0:T(8,128)}, bf16[512,1024]{1,0:T(8,128)(2,1)}, f32[2048,512]{1,0:T(8,128)}) custom-call(f32[512,512]{1,0:T(8,128)} %get-tuple-element.118.q_ref, f32[512,1024]{1,0:T(8,128)} %get-tuple-element.115.og_ref, f32[512,512]{1,0:T(8,128)} %get-tuple-element.116.ld_ref, f32[512,1024]{1,0:T(8,128)} %local.1.within_ref, ...), custom_call_target="tpu_custom_call" | custom-call | bytes 39000000 | tf_op jit(solution)/shard_map/attend/pallas_call | solution.py:323
  77.1 26.7 %mlp.1 = (bf16[512,1024]{1,0:T(8,128)(2,1)}, f32[512,1024]{1,0:T(8,128)}, bf16[512,2816]{1,0:T(8,128)(2,1)}, f32[512,2816]{1,0:T(8,128)}, f32[2816,512]{1,0:T(8,128)}) custom-call(s32[96]{0:T(128)} %dynamic-slice_bitcast_fusion.table_ref.core_ref, bf16[512,1024]{1,0:T(8,128)(2,1)} %get-tuple-element.130.mlp_ref, f32[512,2816]{1,0:T(8,128)} %hidden_grad.1.dh_ref, ...), custom_call_target="tpu_custom_call" | custom-call | bytes 90000000 | tf_op jit(solution)/shard_map/mlp/pallas_call | solution.py:384
  103.8 1.9 collective-permute-start.2
  106.2 16.1 %back.1 = (f32[512,1024]{1,0:T(8,128)}, bf16[512,1024]{1,0:T(8,128)(2,1)}, f32[1,1024]{1,0:T(1,128)}, f32[1,256]{1,0:T(1,128)}, f32[512,1024]{1,0:T(8,128)}, /*i...) custom-call(s32[96]{0:T(128)} %dynamic-slice_bitcast_fusion.table_ref.core_r, ...), custom_call_target="tpu_custom_call" | custom-call | bytes 90000000 | tf_op jit(solution)/shard_map/back/pallas_call | solution.py:564
  122.3 4.8 %all-to-all-start.2 = ((f32[16,128,128]{2,1,0:T(8,128)}), f32[16,128,128]{2,1,0:T(8,128)}, u32[]{:S(2)}, u32[]{:S(2)}) async-start(f32[16,128,128]{2,1,0:T(8,128)} %get-tuple-element.136), calls=%async_computation.2 | async-start | bytes 2097152 | tf_op jit(solution)/shard_map/all_to_all | solution.py:896
  127.7 13.5 %down_grad.1 = (f32[2,16,176,128]{3,2,1,0:T(8,128)}, f32[2,16,176,128]{3,2,1,0:T(8,128)}) custom-call(s32[96]{0:T(128)} %dynamic-slice_bitcast_fusion.table_ref.core_ref, f32[16,176,512]{2,1,0:T(8,128)} %bitcast.39, f32[16,176,512]{2,1,0:T(8,128)} %bitcast.8.hid_other, bf16[512,1024]{1,0:T(8,128)(2,1)} %bitcast.34, f32[512,512]{1,0:T(8,128)} %collective-permute-done.1.cot_other), custom_call_target="tpu_custom_call" | custom-call | bytes 300000 | tf_op jit(solution)/shard_map/down_grad/pallas_call | solution.py:437
  141.3 2.3 all-to-all-done.2.part_ref
  143.6 2.5 collective-permute-start.6
  146.1 2.3 prefix.3
  148.4 4.6 %all-to-all-start.3 = ((f32[16,128,128]{2,1,0:T(8,128)}), f32[16,128,128]{2,1,0:T(8,128)}, u32[]{:S(2)}, u32[]{:S(2)}) async-start(f32[16,128,128]{2,1,0:T(8,128)} %prefix.3), calls=%async_computation.3 | async-start | bytes 2097152 | tf_op jit(solution)/shard_map/all_to_all | solution.py:896
  153.0 16.7 %up_grad.1 = (f32[8,704,128]{2,1,0:T(8,128)}, f32[8,704,128]{2,1,0:T(8,128)}, f32[8,704,128]{2,1,0:T(8,128)}, f32[8,704,128]{2,1,0:T(8,128)}) custom-call(s32[96]{0:T(128)} %dynamic-slice_bitcast_fusion.table_ref.core_ref, f32[2048,512]{1,0:T(8,128)} %get-tuple-element.143.mlpt_ref.refs_0_, f32[2048,512]{1,0:T(8,128)} %collective-permute-done.4.mlpt_other.refs_1_, ...), custom_call_target="tpu_custom_call" | custom-call | bytes 300000 | tf_op jit(solution)/shard_map/up_grad/pallas_call | solution.py:482
  169.8 2.6 collective-permute-start.7
  172.4 2.4 collective-permute-start.8
  174.8 8.7 %outer.2 = (f32[8,256,128]{2,1,0:T(8,128)}, f32[8,256,128]{2,1,0:T(8,128)}, f32[8,256,128]{2,1,0:T(8,128)}, f32[8,256,128]{2,1,0:T(8,128)}) custom-call(s32[96]{0:T(128)} %dynamic-slice_bitcast_fusion.table_ref.core_ref, f32[2048,512]{1,0:T(8,128)} %get-tuple-element.143.mlpt_ref.refs_0_, f32[2048,512]{1,0:T(8,128)} %collective-permute-done.4.mlpt_other.refs_1_, ...), custom_call_target="tpu_custom_call" | custom-call | bytes 300000 | tf_op jit(solution)/shard_map/outer/pallas_call | solution.py:759
  183.5 3.4 halve_x.1
  187.5 18.5 %inner.1 = (bf16[512,2048]{1,0:T(8,128)(2,1)}, f32[512,1024]{1,0:T(8,128)}, bf16[512,16]{1,0:T(8,128)(2,1)}, f32[16,24,128]{2,1,0:T(8,128)}) custom-call(s32[2]{0:T(128)} %limit_ref.1, s32[96]{0:T(128)} %dynamic-slice_bitcast_fusion.table_ref.core_ref, f32[512,512]{1,0:T(8,128)} %get-tuple-element.118.q_ref, f32[512,512]{1,0:T(8,128)} %get-tuple-element.119.k_ref, ...), custom_call_target="tpu_custom_call" | custom-call | bytes 900000000 | tf_op jit(solution)/shard_map/inner/pallas_call | solution.py:678
  206.0 11.2 %input_back.1 = (bf16[512,1024]{1,0:T(8,128)(2,1)}, f32[16,24,128]{2,1,0:T(8,128)}) custom-call(bf16[512,2048]{1,0:T(8,128)(2,1)} %get-tuple-element.160.y_ref.refs_2_, bf16[512,1024]{1,0:T(8,128)(2,1)} %get-tuple-element.149.refs_6_.og_ref, bf16[1024,3072]{1,0:T(8,128)(2,1)} %w_ref.5, bf16[512,16]{1,0:T(8,128)(2,1)} %get-tuple-element.161.dlow_ref, ...), custom_call_target="tpu_custom_call" | custom-call | bytes 36000000 | tf_op jit(solution)/shard_map/input_back/pallas_call | solution.py:813
  217.3 1.2 collective-permute-done.11.refs_5_.refs_6_.refs_7_.refs_8_
  218.7 4.6 %halve.8 = (f32[4,704,128]{2,1,0:T(8,128)}, f32[4,704,128]{2,1,0:T(8,128)}) custom-call(s32[96]{0:T(128)} %dynamic-slice_bitcast_fusion.table_ref.core_ref, f32[8,704,128]{2,1,0:T(8,128)} %get-tuple-element.179.refs_0_, f32[8,704,128]{2,1,0:T(8,128)} %collective-permute-done.7.refs_1_, f32[8,704,128]{2,1,0:T(8,128)} %get-tuple-element.169.refs_2_.refs_3_.refs_4_.refs_5_, ...), custom_call_target="tpu_custom_call" | custom-call | bytes 300000 | tf_op jit(solution)/shard_map/halve/pallas_call | solution.py:984
  223.3 1.4 collective-permute-start.13
  224.7 1.2 collective-permute-start.14
  225.9 9.9 %outer.3 = (f32[8,344,128]{2,1,0:T(8,128)}, f32[8,344,128]{2,1,0:T(8,128)}, f32[8,368,128]{2,1,0:T(8,128)}, f32[8,368,128]{2,1,0:T(8,128)}) custom-call(s32[96]{0:T(128)} %dynamic-slice_bitcast_fusion.table_ref.core_ref, f32[1024,512]{1,0:T(8,128)} %get-tuple-element.127.refs_4_.refs_0_, f32[1024,512]{1,0:T(8,128)} %collective-permute-done.refs_5_.refs_1_, ...), custom_call_target="tpu_custom_call" | custom-call | bytes 300000 | tf_op jit(solution)/shard_map/outer/pallas_call | solution.py:759
  235.8 1.8 collective-permute-start.17
  237.7 1.8 collective-permute-start.16
  239.4 2.3 collective-permute-done.13.refs_2_
  241.8 2.4 collective-permute-done.14.refs_5_.refs_6_.refs_7_
  244.2 4.1 %halve.9 = (f32[2,704,128]{2,1,0:T(8,128)}, f32[2,704,128]{2,1,0:T(8,128)}) custom-call(s32[96]{0:T(128)} %dynamic-slice_bitcast_fusion.table_ref.core_ref, f32[8,704,128]{2,1,0:T(8,128)} %get-tuple-element.179.refs_0_, f32[8,704,128]{2,1,0:T(8,128)} %collective-permute-done.7.refs_1_, f32[4,704,128]{2,1,0:T(8,128)} %collective-permute-done.13.refs_2_, ...), custom_call_target="tpu_custom_call" | custom-call | bytes 300000 | tf_op jit(solution)/shard_map/halve/pallas_call | solution.py:984
  248.2 4.3 %collective-permute-start.15 = (f32[2,704,128]{2,1,0:T(8,128)}, f32[2,704,128]{2,1,0:T(8,128)}, u32[]{:S(2)}, u32[]{:S(2)}) collective-permute-start(f32[2,704,128]{2,1,0:T(8,128)} %get-tuple-element.181), channel_id=1, source_target_pairs={{0,1},{1,0},{2,3},{3,2},{4,5},{5,4},{6,7},{7,6},{8,9},{9,8},{10,11... | collective-permute-start | bytes 2162696 | tf_op jit(solution)/shard_map/ppermute | solution.py:998
  252.6 3.4 collective-permute-start.18
  255.9 2.7 collective-permute-done.16.refs_3_
  258.6 3.7 %collective-permute-done.17.refs_7_.refs_8_.refs_9_.refs_10_ = f32[8,368,128]{2,1,0:T(8,128)} collective-permute-done((f32[8,368,128]{2,1,0:T(8,128)}, f32[8,368,128]{2,1,0:T(8,128)}, u32[]{:S(2)}, u32[]{:S(2)}) %collective-permute-start.17) | collective-permute-done | bytes 1507360 | tf_op jit(solution)/shard_map/ppermute | solution.py:998
  262.3 4.3 %halve.10 = (f32[4,600,128]{2,1,0:T(8,128)}, f32[4,624,128]{2,1,0:T(8,128)}) custom-call(s32[96]{0:T(128)} %dynamic-slice_bitcast_fusion.table_ref.core_ref, f32[8,256,128]{2,1,0:T(8,128)} %get-tuple-element.182.refs_0_, f32[8,256,128]{2,1,0:T(8,128)} %collective-permute-done.10.refs_1_, f32[8,344,128]{2,1,0:T(8,128)} %get-tuple-element.178.refs_2_, ...), custom_call_target="tpu_custom_call" | custom-call | bytes 300000 | tf_op jit(solution)/shard_map/halve/pallas_call | solution.py:984
  266.9 5.1 %collective-permute-done.15.refs_3_ = f32[2,704,128]{2,1,0:T(8,128)} collective-permute-done((f32[2,704,128]{2,1,0:T(8,128)}, f32[2,704,128]{2,1,0:T(8,128)}, u32[]{:S(2)}, u32[]{:S(2)}) %collective-permute-start.15) | collective-permute-done | bytes 720928 | tf_op jit(solution)/shard_map/ppermute | solution.py:998
  271.9 3.3 halve.11
  275.3 11.9 %collective-permute-done.19.refs_4_ = f32[1,704,128]{2,1,0:T(8,128)} collective-permute-done((f32[1,704,128]{2,1,0:T(8,128)}, f32[1,704,128]{2,1,0:T(8,128)}, u32[]{:S(2)}, u32[]{:S(2)}) %collective-permute-start.19) | collective-permute-done | bytes 360480 | tf_op jit(solution)/shard_map/ppermute | solution.py:998
  287.2 3.6 %halve.12 = f32[1,1408,128]{2,1,0:T(8,128)} custom-call(s32[96]{0:T(128)} %dynamic-slice_bitcast_fusion.table_ref.core_ref, f32[8,704,128]{2,1,0:T(8,128)} %get-tuple-element.179.refs_0_, f32[8,704,128]{2,1,0:T(8,128)} %collective-permute-done.7.refs_1_, f32[4,704,128]{2,1,0:T(8,128)} %collective-permute-done.13.refs_2_, ...), custom_call_target="tpu_custom_call" | custom-call | bytes 300000 | tf_op jit(solution)/shard_map/halve/pallas_call | solution.py:984
  291.7 3.8 %halve.13 = (f32[2,600,128]{2,1,0:T(8,128)}, f32[2,624,128]{2,1,0:T(8,128)}) custom-call(s32[96]{0:T(128)} %dynamic-slice_bitcast_fusion.table_ref.core_ref, f32[8,256,128]{2,1,0:T(8,128)} %get-tuple-element.182.refs_0_, f32[8,256,128]{2,1,0:T(8,128)} %collective-permute-done.10.refs_1_, f32[8,344,128]{2,1,0:T(8,128)} %get-tuple-element.178.refs_2_, ...), custom_call_target="tpu_custom_call" | custom-call | bytes 300000 | tf_op jit(solution)/shard_map/halve/pallas_call | solution.py:984
  295.5 2.4 collective-permute-start.26
  298.6 3.9 %collective-permute-done.21 = f32[1408,128]{1,0:T(8,128)} collective-permute-done((f32[1408,128]{1,0:T(8,128)}, f32[1408,128]{1,0:T(8,128)}, u32[]{:S(2)}, u32[]{:S(2)}) %collective-permute-start.21) | collective-permute-done | bytes 720928 | tf_op jit(solution)/shard_map/ppermute | solution.py:1006
  302.5 2.3 bitcast_add_fusion
  304.8 1.3 collective-permute-done.26.refs_5_
  306.1 2.7 collective-permute-done.27.refs_11_.refs_12_
  308.7 3.2 halve.14
  312.0 3.5 collective-permute-done.22
  315.5 2.3 add.21.a_ref
  318.4 3.5 halve.15
  322.9 8.7 %collective-permute-done.30 = f32[1224,128]{1,0:T(8,128)S(1)} collective-permute-done((f32[1224,128]{1,0:T(8,128)}, f32[1224,128]{1,0:T(8,128)S(1)}, u32[]{:S(2)}, u32[]{:S(2)}) %collective-permute-start.30) | collective-permute-done | bytes 626720 | tf_op jit(solution)/shard_map/ppermute | solution.py:1006
  332.7 1.9 collective-permute-start.31
  334.6 9.5 %collective-permute-done.31 = f32[1400,128]{1,0:T(8,128)S(1)} collective-permute-done((f32[1400,128]{1,0:T(8,128)S(1)}, f32[1400,128]{1,0:T(8,128)S(1)}, u32[]{:S(2)}, u32[]{:S(2)}) %collective-permute-start.31) | collective-permute-done | bytes 716832 | tf_op jit(solution)/shard_map/ppermute | solution.py:1006
  345.2 5.2 %collective-permute-start.32 = (f32[1752,128]{1,0:T(8,128)S(1)}, f32[1752,128]{1,0:T(8,128)}, u32[]{:S(2)}, u32[]{:S(2)}) collective-permute-start(f32[1752,128]{1,0:T(8,128)S(1)} %pad_maximum_fusion.b_ref), channel_id=1, source_target_pairs={{0,16},{16,0},{32,48},{48,32},{64,80},{80,64},{96,112},{112,96},{1... | collective-permute-start | bytes 2691080 | tf_op jit(solution)/shard_map/ppermute | solution.py:900
  350.5 3.0 collective-permute-done.23.a_other
  354.3 3.7 %unpack.1 = (f32[64,5632]{1,0:T(8,128)}, f32[176,1024]{1,0:T(8,128)}, f32[64,1024]{1,0:T(8,128)}, f32[64,3072]{1,0:T(8,128)}, f32[16,64]{1,0:T(8,128)}, /*index=...) custom-call(s32[96]{0:T(128)} %dynamic-slice_bitcast_fusion.table_ref.core_ref, ...), custom_call_target="tpu_custom_call" | custom-call | bytes 12000000 | tf_op jit(solution)/shard_map/unpack/pallas_call | solution.py:1056
  (59 shorter events, 10.4 us)
Async XLA Ops:
  15.3 25.4 %all-to-all-start = ((f32[16,136,128]{2,1,0:T(8,128)}), f32[16,136,128]{2,1,0:T(8,128)}, u32[]{:S(2)}, u32[]{:S(2)}) async-start(f32[16,136,128]{2,1,0:T(8,128)} %get-tuple-element.112), calls=%async_computation | async-start | bytes 2228224 | tf_op jit(solution)/shard_map/all_to_all | solution.py:896
  43.0 7.1 %copy-start.4 = (bf16[256]{0:T(256)(128)(2,1)S(1)}, bf16[256]{0:T(256)(128)(2,1)}, u32[]{:S(2)}) copy-start(bf16[256]{0:T(256)(128)(2,1)} %param.22) | copy-start | bytes 1540
  43.0 7.7 %copy-start.3 = (bf16[1024]{0:T(1024)(128)(2,1)S(1)}, bf16[1024]{0:T(1024)(128)(2,1)}, u32[]{:S(2)}) copy-start(bf16[1024]{0:T(1024)(128)(2,1)} %param.24) | copy-start | bytes 6148
  43.0 34.1 %collective-permute-start = (f32[1024,512]{1,0:T(8,128)}, f32[1024,512]{1,0:T(8,128)}, u32[]{:S(2)}, u32[]{:S(2)}) collective-permute-start(f32[1024,512]{1,0:T(8,128)} %get-tuple-element.127.refs_4_.refs_0_), channel_id=1, source_target_pairs={{0,16},{16,0},{32,48},{48,32},{64,80},{80,64},{96,112},{112,96},{1... | collective-permute-start | bytes 6291464 | tf_op jit(solution)/shard_map/ppermute | solution.py:900
  45.7 31.4 %collective-permute-start.1 = (f32[512,512]{1,0:T(8,128)}, f32[512,512]{1,0:T(8,128)}, u32[]{:S(2)}, u32[]{:S(2)}) collective-permute-start(f32[512,512]{1,0:T(8,128)} %get-tuple-element.129), channel_id=1, source_target_pairs={{0,16},{16,0},{32,48},{48,32},{64,80},{80,64},{96,112},{112,96},{1... | collective-permute-start | bytes 3145736 | tf_op jit(solution)/shard_map/ppermute | solution.py:900
  45.8 21.1 %all-to-all-start.1 = ((f32[16,128,128]{2,1,0:T(8,128)}), f32[16,128,128]{2,1,0:T(8,128)}, u32[]{:S(2)}, u32[]{:S(2)}) async-start(f32[16,128,128]{2,1,0:T(8,128)} %prefix.2), calls=%async_computation.1 | async-start | bytes 2097152 | tf_op jit(solution)/shard_map/all_to_all | solution.py:896
  103.8 23.9 %collective-permute-start.2 = (f32[2816,512]{1,0:T(8,128)}, f32[2816,512]{1,0:T(8,128)}, u32[]{:S(2)}, u32[]{:S(2)}) collective-permute-start(f32[2816,512]{1,0:T(8,128)} %get-tuple-element.138), channel_id=1, source_target_pairs={{0,16},{16,0},{32,48},{48,32},{64,80},{80,64},{96,112},{112,96},{1... | collective-permute-start | bytes 17301512 | tf_op jit(solution)/shard_map/ppermute | solution.py:900
  105.7 47.3 %collective-permute-start.5 = (f32[512,2816]{1,0:T(8,128)}, f32[512,2816]{1,0:T(8,128)}, u32[]{:S(2)}, u32[]{:S(2)}) collective-permute-start(f32[512,2816]{1,0:T(8,128)} %get-tuple-element.145), channel_id=1, source_target_pairs={{0,16},{16,0},{32,48},{48,32},{64,80},{80,64},{96,112},{112,96},{1... | collective-permute-start | bytes 17301512 | tf_op jit(solution)/shard_map/ppermute | solution.py:900
  106.0 47.0 %collective-permute-start.4 = (f32[2048,512]{1,0:T(8,128)}, f32[2048,512]{1,0:T(8,128)}, u32[]{:S(2)}, u32[]{:S(2)}) collective-permute-start(f32[2048,512]{1,0:T(8,128)} %get-tuple-element.143.mlpt_ref.refs_0_), channel_id=1, source_target_pairs={{0,16},{16,0},{32,48},{48,32},{64,80},{80,64},{96,112},{112,96},{1... | collective-permute-start | bytes 12582920 | tf_op jit(solution)/shard_map/ppermute | solution.py:900
  122.3 21.3 %all-to-all-start.2 = ((f32[16,128,128]{2,1,0:T(8,128)}), f32[16,128,128]{2,1,0:T(8,128)}, u32[]{:S(2)}, u32[]{:S(2)}) async-start(f32[16,128,128]{2,1,0:T(8,128)} %get-tuple-element.136), calls=%async_computation.2 | async-start | bytes 2097152 | tf_op jit(solution)/shard_map/all_to_all | solution.py:896
  127.1 25.9 %collective-permute-start.3 = (f32[512,1024]{1,0:T(8,128)}, f32[512,1024]{1,0:T(8,128)}, u32[]{:S(2)}, u32[]{:S(2)}) collective-permute-start(f32[512,1024]{1,0:T(8,128)} %get-tuple-element.142), channel_id=1, source_target_pairs={{0,16},{16,0},{32,48},{48,32},{64,80},{80,64},{96,112},{112,96},{1... | collective-permute-start | bytes 6291464 | tf_op jit(solution)/shard_map/ppermute | solution.py:900
  143.6 39.9 %collective-permute-start.6 = (f32[2,2816,128]{2,1,0:T(8,128)}, f32[2,2816,128]{2,1,0:T(8,128)}, u32[]{:S(2)}, u32[]{:S(2)}) collective-permute-start(f32[2,2816,128]{2,1,0:T(8,128)} %bitcast.46), channel_id=1, source_target_pairs={{0,32},{16,112},{32,0},{48,80},{64,96},{80,48},{96,64},{112,16},{1... | collective-permute-start | bytes 8650760 | tf_op jit(solution)/shard_map/ppermute | solution.py:1006
  148.4 21.4 %all-to-all-start.3 = ((f32[16,128,128]{2,1,0:T(8,128)}), f32[16,128,128]{2,1,0:T(8,128)}, u32[]{:S(2)}, u32[]{:S(2)}) async-start(f32[16,128,128]{2,1,0:T(8,128)} %prefix.3), calls=%async_computation.3 | async-start | bytes 2097152 | tf_op jit(solution)/shard_map/all_to_all | solution.py:896
  169.8 48.7 %collective-permute-start.7 = (f32[8,704,128]{2,1,0:T(8,128)}, f32[8,704,128]{2,1,0:T(8,128)}, u32[]{:S(2)}, u32[]{:S(2)}) collective-permute-start(f32[8,704,128]{2,1,0:T(8,128)} %get-tuple-element.168), channel_id=1, source_target_pairs={{0,4},{1,5},{2,6},{3,7},{4,0},{5,1},{6,2},{7,3},{8,12},{9,13},{10,... | collective-permute-start | bytes 8650760 | tf_op jit(solution)/shard_map/ppermute | solution.py:998
  172.4 46.1 %collective-permute-start.8 = (f32[8,704,128]{2,1,0:T(8,128)}, f32[8,704,128]{2,1,0:T(8,128)}, u32[]{:S(2)}, u32[]{:S(2)}) collective-permute-start(f32[8,704,128]{2,1,0:T(8,128)} %get-tuple-element.171), channel_id=1, source_target_pairs={{0,1},{1,0},{2,3},{3,2},{4,5},{5,4},{6,7},{7,6},{8,9},{9,8},{10,11... | collective-permute-start | bytes 8650760 | tf_op jit(solution)/shard_map/ppermute | solution.py:998
  186.9 31.6 %collective-permute-start.9 = (f32[1,2816,128]{2,1,0:T(8,128)}, f32[1,2816,128]{2,1,0:T(8,128)}, u32[]{:S(2)}, u32[]{:S(2)}) collective-permute-start(f32[1,2816,128]{2,1,0:T(8,128)} %halve_x.1), channel_id=1, source_target_pairs={{0,96},{16,48},{32,64},{48,16},{64,32},{80,112},{96,0},{112,80},{1... | collective-permute-start | bytes 4325384 | tf_op jit(solution)/shard_map/ppermute | solution.py:1006
  186.9 30.4 %collective-permute-start.10 = (f32[8,256,128]{2,1,0:T(8,128)}, f32[8,256,128]{2,1,0:T(8,128)}, u32[]{:S(2)}, u32[]{:S(2)}) collective-permute-start(f32[8,256,128]{2,1,0:T(8,128)} %get-tuple-element.175), channel_id=1, source_target_pairs={{0,4},{1,5},{2,6},{3,7},{4,0},{5,1},{6,2},{7,3},{8,12},{9,13},{10,... | collective-permute-start | bytes 3145736 | tf_op jit(solution)/shard_map/ppermute | solution.py:998
  187.1 31.3 %collective-permute-start.11 = (f32[8,256,128]{2,1,0:T(8,128)}, f32[8,256,128]{2,1,0:T(8,128)}, u32[]{:S(2)}, u32[]{:S(2)}) collective-permute-start(f32[8,256,128]{2,1,0:T(8,128)} %get-tuple-element.176), channel_id=1, source_target_pairs={{0,1},{1,0},{2,3},{3,2},{4,5},{5,4},{6,7},{7,6},{8,9},{9,8},{10,11... | collective-permute-start | bytes 3145736 | tf_op jit(solution)/shard_map/ppermute | solution.py:998
  218.5 7.5 %collective-permute-start.12 = (f32[512,1024]{1,0:T(8,128)}, f32[512,1024]{1,0:T(8,128)}, u32[]{:S(2)}, u32[]{:S(2)}) collective-permute-start(f32[512,1024]{1,0:T(8,128)} %get-tuple-element.177), channel_id=1, source_target_pairs={{0,16},{16,0},{32,48},{48,32},{64,80},{80,64},{96,112},{112,96},{1... | collective-permute-start | bytes 6291464 | tf_op jit(solution)/shard_map/ppermute | solution.py:900
  223.3 18.5 %collective-permute-start.13 = (f32[4,704,128]{2,1,0:T(8,128)}, f32[4,704,128]{2,1,0:T(8,128)}, u32[]{:S(2)}, u32[]{:S(2)}) collective-permute-start(f32[4,704,128]{2,1,0:T(8,128)} %get-tuple-element.172), channel_id=1, source_target_pairs={{0,12},{1,13},{2,14},{3,15},{4,8},{5,9},{6,10},{7,11},{8,4},{9,5},... | collective-permute-start | bytes 4325384 | tf_op jit(solution)/shard_map/ppermute | solution.py:998
  224.7 19.4 %collective-permute-start.14 = (f32[4,704,128]{2,1,0:T(8,128)}, f32[4,704,128]{2,1,0:T(8,128)}, u32[]{:S(2)}, u32[]{:S(2)}) collective-permute-start(f32[4,704,128]{2,1,0:T(8,128)} %get-tuple-element.180), channel_id=1, source_target_pairs={{0,3},{1,2},{2,1},{3,0},{4,7},{5,6},{6,5},{7,4},{8,11},{9,10},{10,... | collective-permute-start | bytes 4325384 | tf_op jit(solution)/shard_map/ppermute | solution.py:998
  235.8 26.5 %collective-permute-start.17 = (f32[8,368,128]{2,1,0:T(8,128)}, f32[8,368,128]{2,1,0:T(8,128)}, u32[]{:S(2)}, u32[]{:S(2)}) collective-permute-start(f32[8,368,128]{2,1,0:T(8,128)} %get-tuple-element.186), channel_id=1, source_target_pairs={{0,1},{1,0},{2,3},{3,2},{4,5},{5,4},{6,7},{7,6},{8,9},{9,8},{10,11... | collective-permute-start | bytes 4521992 | tf_op jit(solution)/shard_map/ppermute | solution.py:998
  237.7 20.9 %collective-permute-start.16 = (f32[8,344,128]{2,1,0:T(8,128)}, f32[8,344,128]{2,1,0:T(8,128)}, u32[]{:S(2)}, u32[]{:S(2)}) collective-permute-start(f32[8,344,128]{2,1,0:T(8,128)} %get-tuple-element.183), channel_id=1, source_target_pairs={{0,4},{1,5},{2,6},{3,7},{4,0},{5,1},{6,2},{7,3},{8,12},{9,13},{10,... | collective-permute-start | bytes 4227080 | tf_op jit(solution)/shard_map/ppermute | solution.py:998
  248.2 23.7 %collective-permute-start.15 = (f32[2,704,128]{2,1,0:T(8,128)}, f32[2,704,128]{2,1,0:T(8,128)}, u32[]{:S(2)}, u32[]{:S(2)}) collective-permute-start(f32[2,704,128]{2,1,0:T(8,128)} %get-tuple-element.181), channel_id=1, source_target_pairs={{0,1},{1,0},{2,3},{3,2},{4,5},{5,4},{6,7},{7,6},{8,9},{9,8},{10,11... | collective-permute-start | bytes 2162696 | tf_op jit(solution)/shard_map/ppermute | solution.py:998
  252.6 19.4 %collective-permute-start.18 = (f32[2,704,128]{2,1,0:T(8,128)}, f32[2,704,128]{2,1,0:T(8,128)}, u32[]{:S(2)}, u32[]{:S(2)}) collective-permute-start(f32[2,704,128]{2,1,0:T(8,128)} %get-tuple-element.189), channel_id=1, source_target_pairs={{0,4},{1,5},{2,6},{3,7},{4,0},{5,1},{6,2},{7,3},{8,12},{9,13},{10,... | collective-permute-start | bytes 2162696 | tf_op jit(solution)/shard_map/ppermute | solution.py:998
  266.6 25.1 %collective-permute-start.25 = (f32[4,624,128]{2,1,0:T(8,128)}, f32[4,624,128]{2,1,0:T(8,128)}, u32[]{:S(2)}, u32[]{:S(2)}) collective-permute-start(f32[4,624,128]{2,1,0:T(8,128)} %get-tuple-element.194), channel_id=1, source_target_pairs={{0,3},{1,2},{2,1},{3,0},{4,7},{5,6},{6,5},{7,4},{8,11},{9,10},{10,... | collective-permute-start | bytes 3833864 | tf_op jit(solution)/shard_map/ppermute | solution.py:998
  266.9 24.9 %collective-permute-start.24 = (f32[4,600,128]{2,1,0:T(8,128)}, f32[4,600,128]{2,1,0:T(8,128)}, u32[]{:S(2)}, u32[]{:S(2)}) collective-permute-start(f32[4,600,128]{2,1,0:T(8,128)} %get-tuple-element.187), channel_id=1, source_target_pairs={{0,12},{1,13},{2,14},{3,15},{4,8},{5,9},{6,10},{7,11},{8,4},{9,5},... | collective-permute-start | bytes 3686408 | tf_op jit(solution)/shard_map/ppermute | solution.py:998
  275.2 11.9 %collective-permute-start.19 = (f32[1,704,128]{2,1,0:T(8,128)}, f32[1,704,128]{2,1,0:T(8,128)}, u32[]{:S(2)}, u32[]{:S(2)}) collective-permute-start(f32[1,704,128]{2,1,0:T(8,128)} %get-tuple-element.190), channel_id=1, source_target_pairs={{0,3},{1,2},{2,1},{3,0},{4,7},{5,6},{6,5},{7,4},{8,11},{9,10},{10,... | collective-permute-start | bytes 1081352 | tf_op jit(solution)/shard_map/ppermute | solution.py:998
  275.3 11.9 %collective-permute-start.20 = (f32[1,704,128]{2,1,0:T(8,128)}, f32[1,704,128]{2,1,0:T(8,128)}, u32[]{:S(2)}, u32[]{:S(2)}) collective-permute-start(f32[1,704,128]{2,1,0:T(8,128)} %get-tuple-element.191), channel_id=1, source_target_pairs={{0,12},{1,13},{2,14},{3,15},{4,8},{5,9},{6,10},{7,11},{8,4},{9,5},... | collective-permute-start | bytes 1081352 | tf_op jit(solution)/shard_map/ppermute | solution.py:998
  290.8 11.7 %collective-permute-start.21 = (f32[1408,128]{1,0:T(8,128)}, f32[1408,128]{1,0:T(8,128)}, u32[]{:S(2)}, u32[]{:S(2)}) collective-permute-start(f32[1408,128]{1,0:T(8,128)} %bitcast.40), channel_id=1, source_target_pairs={{0,32},{16,112},{32,0},{48,80},{64,96},{80,48},{96,64},{112,16},{1... | collective-permute-start | bytes 2162696 | tf_op jit(solution)/shard_map/ppermute | solution.py:1006
  295.5 10.5 %collective-permute-start.26 = (f32[2,600,128]{2,1,0:T(8,128)}, f32[2,600,128]{2,1,0:T(8,128)}, u32[]{:S(2)}, u32[]{:S(2)}) collective-permute-start(f32[2,600,128]{2,1,0:T(8,128)} %get-tuple-element.195), channel_id=1, source_target_pairs={{0,1},{1,0},{2,3},{3,2},{4,5},{5,4},{6,7},{7,6},{8,9},{9,8},{10,11... | collective-permute-start | bytes 1843208 | tf_op jit(solution)/shard_map/ppermute | solution.py:998
  297.9 10.8 %collective-permute-start.27 = (f32[2,624,128]{2,1,0:T(8,128)}, f32[2,624,128]{2,1,0:T(8,128)}, u32[]{:S(2)}, u32[]{:S(2)}) collective-permute-start(f32[2,624,128]{2,1,0:T(8,128)} %get-tuple-element.197), channel_id=1, source_target_pairs={{0,4},{1,5},{2,6},{3,7},{4,0},{5,1},{6,2},{7,3},{8,12},{9,13},{10,... | collective-permute-start | bytes 1916936 | tf_op jit(solution)/shard_map/ppermute | solution.py:998
  304.8 10.7 %collective-permute-start.22 = (f32[1408,128]{1,0:T(8,128)}, f32[1408,128]{1,0:T(8,128)}, u32[]{:S(2)}, u32[]{:S(2)}) collective-permute-start(f32[1408,128]{1,0:T(8,128)} %bitcast_add_fusion), channel_id=1, source_target_pairs={{0,96},{16,48},{32,64},{48,16},{64,32},{80,112},{96,0},{112,80},{1... | collective-permute-start | bytes 2162696 | tf_op jit(solution)/shard_map/ppermute | solution.py:1006
  312.0 6.4 %collective-permute-start.29 = (f32[1,624,128]{2,1,0:T(8,128)}, f32[1,624,128]{2,1,0:T(8,128)}, u32[]{:S(2)}, u32[]{:S(2)}) collective-permute-start(f32[1,624,128]{2,1,0:T(8,128)} %get-tuple-element.199), channel_id=1, source_target_pairs={{0,12},{1,13},{2,14},{3,15},{4,8},{5,9},{6,10},{7,11},{8,4},{9,5},... | collective-permute-start | bytes 958472 | tf_op jit(solution)/shard_map/ppermute | solution.py:998
  312.0 6.4 %collective-permute-start.28 = (f32[1,600,128]{2,1,0:T(8,128)}, f32[1,600,128]{2,1,0:T(8,128)}, u32[]{:S(2)}, u32[]{:S(2)}) collective-permute-start(f32[1,600,128]{2,1,0:T(8,128)} %get-tuple-element.198), channel_id=1, source_target_pairs={{0,3},{1,2},{2,1},{3,0},{4,7},{5,6},{6,5},{7,4},{8,11},{9,10},{10,... | collective-permute-start | bytes 921608 | tf_op jit(solution)/shard_map/ppermute | solution.py:998
  321.9 9.6 %collective-permute-start.30 = (f32[1224,128]{1,0:T(8,128)}, f32[1224,128]{1,0:T(8,128)S(1)}, u32[]{:S(2)}, u32[]{:S(2)}) collective-permute-start(f32[1224,128]{1,0:T(8,128)} %bitcast.41), channel_id=1, source_target_pairs={{0,96},{16,48},{32,64},{48,16},{64,32},{80,112},{96,0},{112,80},{1... | collective-permute-start | bytes 1880072 | tf_op jit(solution)/shard_map/ppermute | solution.py:1006
  332.7 17.7 %copy-start.1 = (f32[1408,128]{1,0:T(8,128)S(1)}, f32[1408,128]{1,0:T(8,128)}, u32[]{:S(2)}) copy-start(f32[1408,128]{1,0:T(8,128)} %add.21.a_ref) | copy-start | bytes 2162692
  332.7 11.4 %collective-permute-start.31 = (f32[1400,128]{1,0:T(8,128)S(1)}, f32[1400,128]{1,0:T(8,128)S(1)}, u32[]{:S(2)}, u32[]{:S(2)}) collective-permute-start(f32[1400,128]{1,0:T(8,128)S(1)} %pad_maximum_fusion.1), channel_id=1, source_target_pairs={{0,32},{16,112},{32,0},{48,80},{64,96},{80,48},{96,64},{112,16},{1... | collective-permute-start | bytes 2150408 | tf_op jit(solution)/shard_map/ppermute | solution.py:1006
  344.3 0.9 copy-start
  345.2 9.1 %collective-permute-start.32 = (f32[1752,128]{1,0:T(8,128)S(1)}, f32[1752,128]{1,0:T(8,128)}, u32[]{:S(2)}, u32[]{:S(2)}) collective-permute-start(f32[1752,128]{1,0:T(8,128)S(1)} %pad_maximum_fusion.b_ref), channel_id=1, source_target_pairs={{0,16},{16,0},{32,48},{48,32},{64,80},{80,64},{96,112},{112,96},{1... | collective-permute-start | bytes 2691080 | tf_op jit(solution)/shard_map/ppermute | solution.py:900
  350.5 3.0 collective-permute-start.23
  353.4 0.9 copy-start.2

commit v2 on v1

--- a/solution.py
+++ b/solution.py
@@ -156,7 +156,7 @@
             grid=(3,),
             in_specs=[
                 full((N, D)), full((1, D)), pl.BlockSpec((D, KD), lambda n, s, c: (0, n + 1)),
-                full((16, D)), full((16, KD)), full((1, KD)),
+                full((16, D)), full((16, KD)), pl.BlockSpec((1, KD), lambda n, s, c: (0, 4)),
             ],
             out_specs=[
                 full((N, KD)), pl.BlockSpec((N, KD), lambda n, s, c: (0, jnp.maximum(n - 1, 0))),
@@ -327,7 +327,8 @@
             rows(KD), rows(VALUE), rows(KD), rows(VALUE), full((8, KD)),
             pl.BlockSpec((1, HEADS, VHEAD, KHEAD), lambda m: (m // 2, 0, 0, 0)),
             pl.BlockSpec((1, 1, HEADS, VHEAD, KHEAD), lambda m: (m // 2, 0, 0, 0, 0)),
-            rows(D), full((VALUE, D)), full((1, VHEAD)), full((1, D)),
+            rows(D), full((VALUE, D)), pl.BlockSpec((1, VHEAD), lambda m: (0, 10)),
+            pl.BlockSpec((1, D), lambda m: (0, 1)),
         ],
         out_specs=[
             rows(VALUE), rows(D), rows(D), pl.BlockSpec((D + VALUE, BLK), lambda m: (0, m)),
@@ -564,7 +565,8 @@
     return pl.pallas_call(
         back_kernel,
         grid_spec=pltpu.PrefetchScalarGridSpec(num_scalar_prefetch=1, grid=(4,), in_specs=[
-            wide, wide, wide, full((1, D)), full((VALUE, D)), full((1, VHEAD)),
+            wide, wide, wide, pl.BlockSpec((1, D), lambda m, c: (0, 1)), full((VALUE, D)),
+            pl.BlockSpec((1, VHEAD), lambda m, c: (0, 10)),
             pl.BlockSpec((BLK, VALUE), lambda m, c: (block(m), 0)),
             pl.BlockSpec((BLK, VALUE), lambda m, c: (block(m), 0)),
             pl.BlockSpec((BLK, KD), lambda m, c: (block(m), 0)),
@@ -1076,12 +1078,12 @@
     table = lax.dynamic_slice(jnp.asarray(TABLE), (device, 0), (1, 96)).reshape(96)
     tok = tokens.reshape(N, D)
     cot = cotangent.reshape(N, D)
-    line = lambda vector: vector.reshape(1, -1)
     flat = lambda value: value.reshape(2, -1, 128)
 
     down_t, up_t = gate_down.T, gate_up.T
+    vectors = jnp.concatenate([norm_gain, mlp_gain, gate_bias, head_gain]).reshape(1, -1)
     k, v, normed, ld, cl, logit, low, upd, pieces = project(
-        lengths, table, tok, line(norm_gain), in_weight, down_t, up_t, line(gate_bias)
+        lengths, table, tok, vectors, in_weight, down_t, up_t, vectors
     )
     gathered = exchange(pieces)
     q, og, normed_t, cot_send = project_rest(table, after(normed, pieces), in_weight, cot)
@@ -1091,14 +1093,14 @@
     d_hidden = hidden_grad(after(cot, within), down_weight)
     incoming = after(exchange(incoming), d_hidden).reshape(ROWS, HEADS, VHEAD, KHEAD)
     heads, middle, mlp_in, joint = attend(
-        q, og, ld, within, cl, incoming, upd, tok, out_weight, line(head_gain), line(mlp_gain)
+        q, og, ld, within, cl, incoming, upd, tok, out_weight, vectors, vectors
     )
     output, dmlp, act, act_send, hidden_t = mlp(
         table, after(mlp_in, normed_other, cot_other), d_hidden, up_weight, down_weight, middle
     )
     hidden_other, act_other, joint_other = swap(hidden_t), swap(act_send), swap(joint)
     dmid, datt, g_mlp_gain, g_head_gain, dheads, dog, sends, adj, pieces_back = back(
-        table, middle, dmlp, cot, line(mlp_gain), out_weight, line(head_gain), heads, og, q, ld, cl
+        table, middle, dmlp, cot, vectors, out_weight, vectors, heads, og, q, ld, cl
     )
     sends_other = swap(sends)
     owned = exchange(pieces_back)
@@ -1127,7 +1129,7 @@
         g_head_gain, g_mlp_gain,
     )
     input_grad, pack = input_back(
-        dproj, dog, in_weight, dlow, down_t, tok, line(norm_gain), dmid, pack
+        dproj, dog, in_weight, dlow, down_t, tok, vectors, dmid, pack
     )
     dproj_got = swap(after(dproj_send, dn_got, pack, *up_gots, *four_got))
     up = [([(after(up_0, pack), up_gots[0])], []), ([(up_1, up_gots[1])], [])]

time: 361 us -> 359 us (level)
  waiting for transfers between devices: 74 us -> 80.9 us
  starting transfers between devices: 61.8 us -> 56.1 us
    ppermute x18, starting transfers between devices: 22.9 us -> 16.8 us  [hop(): return lax.ppermute(value, ('dp', 'seq'), STEPS[v][step])]
    all_to_all x4, waiting for transfers between devices: 11.6 us -> 16.3 us  [exchange(): return lax.all_to_all(value, 'seq', 0, 0, tiled=True)]
  transfers between devices with their start and end apart: 37 -> 37, of which waited for: 19 -> 20; matrix products, arithmetic and copies ran while one was open for 2% -> 2% of each run, Pallas kernels for 45% -> 45%
where the time goes in v2:
time: 359 us; the launch traced here: 357 us
  Pallas kernels  208 us (58%)
  waiting for transfers between devices  80.9 us (23%)
  starting transfers between devices  56.1 us (16%)
  other arithmetic  6.53 us (2%)
  local copies, waits for them, and re-layouts  4.63 us (1%)
    ppermute x18, waiting for transfers between devices, hop(): return lax.ppermute(value, ('dp', 'seq'), STEPS[v][step])  35.5 us
    pallas_call x8, Pallas kernels, halve(): pl.pallas_call(functools.partial(halve_kernel, shapes, moves), grid_spec=...  30.5 us
    pallas_call x1, Pallas kernels, mlp(): pl.pallas_call(mlp_kernel, grid_spec=pltpu.PrefetchScalarGridSpec(num_sca...  26.7 us
    ppermute x6, waiting for transfers between devices, along_x(): return lax.ppermute(value, 'dp', ACROSS[step])  26.1 us
    all_to_all x4, starting transfers between devices, exchange(): return lax.all_to_all(value, 'seq', 0, 0, tiled=True)  21.7 us
    pallas_call x2, Pallas kernels, outer(): pl.pallas_call(functools.partial(outer_kernel, [streams for *_, streams i...  18.6 us
    pallas_call x1, Pallas kernels, inner(): pl.pallas_call(inner_kernel, grid_spec=pltpu.PrefetchScalarGridSpec(num_s...  18.4 us
    ppermute x18, starting transfers between devices, hop(): return lax.ppermute(value, ('dp', 'seq'), STEPS[v][step])  16.8 us
  transfers between devices with their start and end apart: 37, of which 20 were waited for; matrix products, arithmetic and copies ran while one was open for 2% of the time, Pallas kernels for 45%

profile of v2, /device:TPU:1, one launch (start us, length us, event | category | flops | bytes accessed | tf_op | source)
XLA Modules:
  0.0 356.8 jit_solution(1187635620561236596)
XLA Ops:
  2.0 1.3 dynamic-slice_bitcast_fusion.table_ref.core_ref
  3.3 10.9 %project.1 = (f32[512,512]{1,0:T(8,128)}, f32[512,1024]{1,0:T(8,128)}, bf16[512,1024]{1,0:T(8,128)(2,1)}, f32[512,512]{1,0:T(8,128)}, f32[8,512]{1,0:T(8,128)}, ...) custom-call(s32[2]{0:T(128)} %limit_ref.1, ...), custom_call_target="tpu_custom_call" | custom-call | bytes 30000000 | tf_op jit(solution)/shard_map/project/pallas_call | solution.py:152
  14.1 8.7 %all-to-all-start = ((f32[16,136,128]{2,1,0:T(8,128)}), f32[16,136,128]{2,1,0:T(8,128)}, u32[]{:S(2)}, u32[]{:S(2)}) async-start(f32[16,136,128]{2,1,0:T(8,128)} %get-tuple-element.112), calls=%async_computation | async-start | bytes 2228224 | tf_op jit(solution)/shard_map/all_to_all | solution.py:898
  22.8 8.2 %project_rest.1 = (f32[512,512]{1,0:T(8,128)}, f32[512,1024]{1,0:T(8,128)}, f32[1024,512]{1,0:T(8,128)}, f32[512,512]{1,0:T(8,128)}) custom-call(s32[96]{0:T(128)} %dynamic-slice_bitcast_fusion.table_ref.core_ref, bf16[512,1024]{1,0:T(8,128)(2,1)} %get-tuple-element.113.normed_ref, bf16[1024,3072]{1,0:T(8,128)(2,1)} %w_ref.5, bf16[512,1024]{1,0:T(8,128)(2,1)} %bitcast.31), custom_call_target="tpu_custom_call" | custom-call | bytes 300000 | tf_op jit(solution)/shard_map/project_rest/pallas_call | solution.py:203
  31.0 8.6 %all-to-all-done.part_ref.decay_ref = f32[16,136,128]{2,1,0:T(8,128)} async-done(((f32[16,136,128]{2,1,0:T(8,128)}), f32[16,136,128]{2,1,0:T(8,128)}, u32[]{:S(2)}, u32[]{:S(2)}) %all-to-all-start) | async-done | bytes 1114144 | tf_op jit(solution)/shard_map/all_to_all | solution.py:898
  39.6 2.3 prefix.2
  41.8 2.7 collective-permute-start
  44.5 4.3 %all-to-all-start.1 = ((f32[16,128,128]{2,1,0:T(8,128)}), f32[16,128,128]{2,1,0:T(8,128)}, u32[]{:S(2)}, u32[]{:S(2)}) async-start(f32[16,128,128]{2,1,0:T(8,128)} %prefix.2), calls=%async_computation.1 | async-start | bytes 2097152 | tf_op jit(solution)/shard_map/all_to_all | solution.py:898
  48.9 7.6 %local.1.within_ref = f32[512,1024]{1,0:T(8,128)} custom-call(f32[512,512]{1,0:T(8,128)} %get-tuple-element.118.q_ref, f32[512,512]{1,0:T(8,128)} %get-tuple-element.119.k_ref, f32[512,1024]{1,0:T(8,128)} %get-tuple-element.120.v_ref, f32[512,512]{1,0:T(8,128)} %get-tuple-element.116.ld_ref), custom_call_target="tpu_custom_call" | custom-call | bytes 300000 | tf_op jit(solution)/shard_map/local/pallas_call | solution.py:239
  56.5 7.4 %hidden_grad.1.dh_ref = f32[512,2816]{1,0:T(8,128)} custom-call(bf16[512,1024]{1,0:T(8,128)(2,1)} %bitcast.32, bf16[2816,1024]{1,0:T(8,128)(2,1)} %wd_ref.3), custom_call_target="tpu_custom_call" | custom-call | bytes 300000 | tf_op jit(solution)/shard_map/hidden_grad/pallas_call | solution.py:256
  63.8 1.6 all-to-all-done.1
  65.4 10.2 %attend.1 = (f32[512,1024]{1,0:T(8,128)}, f32[512,1024]{1,0:T(8,128)}, bf16[512,1024]{1,0:T(8,128)(2,1)}, f32[2048,512]{1,0:T(8,128)}) custom-call(f32[512,512]{1,0:T(8,128)} %get-tuple-element.118.q_ref, f32[512,1024]{1,0:T(8,128)} %get-tuple-element.115.og_ref, f32[512,512]{1,0:T(8,128)} %get-tuple-element.116.ld_ref, f32[512,1024]{1,0:T(8,128)} %local.1.within_ref, ...), custom_call_target="tpu_custom_call" | custom-call | bytes 39000000 | tf_op jit(solution)/shard_map/attend/pallas_call | solution.py:323
  75.6 26.7 %mlp.1 = (bf16[512,1024]{1,0:T(8,128)(2,1)}, f32[512,1024]{1,0:T(8,128)}, bf16[512,2816]{1,0:T(8,128)(2,1)}, f32[512,2816]{1,0:T(8,128)}, f32[2816,512]{1,0:T(8,128)}) custom-call(s32[96]{0:T(128)} %dynamic-slice_bitcast_fusion.table_ref.core_ref, bf16[512,1024]{1,0:T(8,128)(2,1)} %get-tuple-element.130.mlp_ref, f32[512,2816]{1,0:T(8,128)} %hidden_grad.1.dh_ref, ...), custom_call_target="tpu_custom_call" | custom-call | bytes 90000000 | tf_op jit(solution)/shard_map/mlp/pallas_call | solution.py:385
  102.3 1.9 collective-permute-start.2
  104.7 16.1 %back.1 = (f32[512,1024]{1,0:T(8,128)}, bf16[512,1024]{1,0:T(8,128)(2,1)}, f32[1,1024]{1,0:T(1,128)}, f32[1,256]{1,0:T(1,128)}, f32[512,1024]{1,0:T(8,128)}, /*i...) custom-call(s32[96]{0:T(128)} %dynamic-slice_bitcast_fusion.table_ref.core_r, ...), custom_call_target="tpu_custom_call" | custom-call | bytes 90000000 | tf_op jit(solution)/shard_map/back/pallas_call | solution.py:565
  120.8 4.3 %all-to-all-start.2 = ((f32[16,128,128]{2,1,0:T(8,128)}), f32[16,128,128]{2,1,0:T(8,128)}, u32[]{:S(2)}, u32[]{:S(2)}) async-start(f32[16,128,128]{2,1,0:T(8,128)} %get-tuple-element.136), calls=%async_computation.2 | async-start | bytes 2097152 | tf_op jit(solution)/shard_map/all_to_all | solution.py:898
  125.5 13.6 %down_grad.1 = (f32[2,16,176,128]{3,2,1,0:T(8,128)}, f32[2,16,176,128]{3,2,1,0:T(8,128)}) custom-call(s32[96]{0:T(128)} %dynamic-slice_bitcast_fusion.table_ref.core_ref, f32[16,176,512]{2,1,0:T(8,128)} %bitcast.39, f32[16,176,512]{2,1,0:T(8,128)} %bitcast.8.hid_other, bf16[512,1024]{1,0:T(8,128)(2,1)} %bitcast.34, f32[512,512]{1,0:T(8,128)} %collective-permute-done.1.cot_other), custom_call_target="tpu_custom_call" | custom-call | bytes 300000 | tf_op jit(solution)/shard_map/down_grad/pallas_call | solution.py:438
  139.1 4.0 %all-to-all-done.2.part_ref = f32[16,128,128]{2,1,0:T(8,128)} async-done(((f32[16,128,128]{2,1,0:T(8,128)}), f32[16,128,128]{2,1,0:T(8,128)}, u32[]{:S(2)}, u32[]{:S(2)}) %all-to-all-start.2) | async-done | bytes 1048608 | tf_op jit(solution)/shard_map/all_to_all | solution.py:898
  143.1 2.5 collective-permute-start.6
  145.6 2.3 prefix.3
  147.9 4.3 %all-to-all-start.3 = ((f32[16,128,128]{2,1,0:T(8,128)}), f32[16,128,128]{2,1,0:T(8,128)}, u32[]{:S(2)}, u32[]{:S(2)}) async-start(f32[16,128,128]{2,1,0:T(8,128)} %prefix.3), calls=%async_computation.3 | async-start | bytes 2097152 | tf_op jit(solution)/shard_map/all_to_all | solution.py:898
  152.2 16.7 %up_grad.1 = (f32[8,704,128]{2,1,0:T(8,128)}, f32[8,704,128]{2,1,0:T(8,128)}, f32[8,704,128]{2,1,0:T(8,128)}, f32[8,704,128]{2,1,0:T(8,128)}) custom-call(s32[96]{0:T(128)} %dynamic-slice_bitcast_fusion.table_ref.core_ref, f32[2048,512]{1,0:T(8,128)} %get-tuple-element.143.mlpt_ref.refs_0_, f32[2048,512]{1,0:T(8,128)} %collective-permute-done.4.mlpt_other.refs_1_, ...), custom_call_target="tpu_custom_call" | custom-call | bytes 300000 | tf_op jit(solution)/shard_map/up_grad/pallas_call | solution.py:483
  169.0 2.1 all-to-all-done.3
  171.0 1.3 collective-permute-start.7
  172.3 1.6 collective-permute-start.8
  173.9 8.7 %outer.2 = (f32[8,256,128]{2,1,0:T(8,128)}, f32[8,256,128]{2,1,0:T(8,128)}, f32[8,256,128]{2,1,0:T(8,128)}, f32[8,256,128]{2,1,0:T(8,128)}) custom-call(s32[96]{0:T(128)} %dynamic-slice_bitcast_fusion.table_ref.core_ref, f32[2048,512]{1,0:T(8,128)} %get-tuple-element.143.mlpt_ref.refs_0_, f32[2048,512]{1,0:T(8,128)} %collective-permute-done.4.mlpt_other.refs_1_, ...), custom_call_target="tpu_custom_call" | custom-call | bytes 300000 | tf_op jit(solution)/shard_map/outer/pallas_call | solution.py:761
  182.7 3.4 halve_x.1
  186.3 2.3 collective-permute-start.11
  188.5 18.4 %inner.1 = (bf16[512,2048]{1,0:T(8,128)(2,1)}, f32[512,1024]{1,0:T(8,128)}, bf16[512,16]{1,0:T(8,128)(2,1)}, f32[16,24,128]{2,1,0:T(8,128)}) custom-call(s32[2]{0:T(128)} %limit_ref.1, s32[96]{0:T(128)} %dynamic-slice_bitcast_fusion.table_ref.core_ref, f32[512,512]{1,0:T(8,128)} %get-tuple-element.118.q_ref, f32[512,512]{1,0:T(8,128)} %get-tuple-element.119.k_ref, ...), custom_call_target="tpu_custom_call" | custom-call | bytes 900000000 | tf_op jit(solution)/shard_map/inner/pallas_call | solution.py:680
  206.9 11.2 %input_back.1 = (bf16[512,1024]{1,0:T(8,128)(2,1)}, f32[16,24,128]{2,1,0:T(8,128)}) custom-call(bf16[512,2048]{1,0:T(8,128)(2,1)} %get-tuple-element.160.y_ref.refs_2_, bf16[512,1024]{1,0:T(8,128)(2,1)} %get-tuple-element.149.refs_6_.og_ref, bf16[1024,3072]{1,0:T(8,128)(2,1)} %w_ref.5, bf16[512,16]{1,0:T(8,128)(2,1)} %get-tuple-element.161.dlow_ref, ...), custom_call_target="tpu_custom_call" | custom-call | bytes 36000000 | tf_op jit(solution)/shard_map/input_back/pallas_call | solution.py:815
  218.5 4.6 %halve.8 = (f32[4,704,128]{2,1,0:T(8,128)}, f32[4,704,128]{2,1,0:T(8,128)}) custom-call(s32[96]{0:T(128)} %dynamic-slice_bitcast_fusion.table_ref.core_ref, f32[8,704,128]{2,1,0:T(8,128)} %get-tuple-element.179.refs_0_, f32[8,704,128]{2,1,0:T(8,128)} %collective-permute-done.7.refs_1_, f32[8,704,128]{2,1,0:T(8,128)} %get-tuple-element.169.refs_2_.refs_3_.refs_4_.refs_5_, ...), custom_call_target="tpu_custom_call" | custom-call | bytes 300000 | tf_op jit(solution)/shard_map/halve/pallas_call | solution.py:986
  223.1 1.2 collective-permute-start.13
  224.4 9.9 %outer.3 = (f32[8,344,128]{2,1,0:T(8,128)}, f32[8,344,128]{2,1,0:T(8,128)}, f32[8,368,128]{2,1,0:T(8,128)}, f32[8,368,128]{2,1,0:T(8,128)}) custom-call(s32[96]{0:T(128)} %dynamic-slice_bitcast_fusion.table_ref.core_ref, f32[1024,512]{1,0:T(8,128)} %get-tuple-element.127.refs_4_.refs_0_, f32[1024,512]{1,0:T(8,128)} %collective-permute-done.refs_5_.refs_1_, ...), custom_call_target="tpu_custom_call" | custom-call | bytes 300000 | tf_op jit(solution)/shard_map/outer/pallas_call | solution.py:761
  234.3 1.8 collective-permute-start.17
  236.1 1.8 collective-permute-start.16
  237.9 4.4 %collective-permute-done.13.refs_2_ = f32[4,704,128]{2,1,0:T(8,128)} collective-permute-done((f32[4,704,128]{2,1,0:T(8,128)}, f32[4,704,128]{2,1,0:T(8,128)}, u32[]{:S(2)}, u32[]{:S(2)}) %collective-permute-start.13) | collective-permute-done | bytes 1441824 | tf_op jit(solution)/shard_map/ppermute | solution.py:1000
  242.3 2.4 collective-permute-done.14.refs_5_.refs_6_.refs_7_
  244.7 4.1 %halve.9 = (f32[2,704,128]{2,1,0:T(8,128)}, f32[2,704,128]{2,1,0:T(8,128)}) custom-call(s32[96]{0:T(128)} %dynamic-slice_bitcast_fusion.table_ref.core_ref, f32[8,704,128]{2,1,0:T(8,128)} %get-tuple-element.179.refs_0_, f32[8,704,128]{2,1,0:T(8,128)} %collective-permute-done.7.refs_1_, f32[4,704,128]{2,1,0:T(8,128)} %collective-permute-done.13.refs_2_, ...), custom_call_target="tpu_custom_call" | custom-call | bytes 300000 | tf_op jit(solution)/shard_map/halve/pallas_call | solution.py:986
  248.8 1.9 collective-permute-start.15
  250.6 2.3 collective-permute-start.18
  253.0 5.6 %collective-permute-done.16.refs_3_ = f32[8,344,128]{2,1,0:T(8,128)} collective-permute-done((f32[8,344,128]{2,1,0:T(8,128)}, f32[8,344,128]{2,1,0:T(8,128)}, u32[]{:S(2)}, u32[]{:S(2)}) %collective-permute-start.16) | collective-permute-done | bytes 1409056 | tf_op jit(solution)/shard_map/ppermute | solution.py:1000
  258.5 2.7 collective-permute-done.17.refs_7_.refs_8_.refs_9_.refs_10_
  261.3 4.3 %halve.10 = (f32[4,600,128]{2,1,0:T(8,128)}, f32[4,624,128]{2,1,0:T(8,128)}) custom-call(s32[96]{0:T(128)} %dynamic-slice_bitcast_fusion.table_ref.core_ref, f32[8,256,128]{2,1,0:T(8,128)} %get-tuple-element.182.refs_0_, f32[8,256,128]{2,1,0:T(8,128)} %collective-permute-done.10.refs_1_, f32[8,344,128]{2,1,0:T(8,128)} %get-tuple-element.178.refs_2_, ...), custom_call_target="tpu_custom_call" | custom-call | bytes 300000 | tf_op jit(solution)/shard_map/halve/pallas_call | solution.py:986
  265.7 4.5 %collective-permute-done.15.refs_3_ = f32[2,704,128]{2,1,0:T(8,128)} collective-permute-done((f32[2,704,128]{2,1,0:T(8,128)}, f32[2,704,128]{2,1,0:T(8,128)}, u32[]{:S(2)}, u32[]{:S(2)}) %collective-permute-start.15) | collective-permute-done | bytes 720928 | tf_op jit(solution)/shard_map/ppermute | solution.py:1000
  270.2 3.3 halve.11
  273.7 12.4 %collective-permute-done.19.refs_4_ = f32[1,704,128]{2,1,0:T(8,128)} collective-permute-done((f32[1,704,128]{2,1,0:T(8,128)}, f32[1,704,128]{2,1,0:T(8,128)}, u32[]{:S(2)}, u32[]{:S(2)}) %collective-permute-start.19) | collective-permute-done | bytes 360480 | tf_op jit(solution)/shard_map/ppermute | solution.py:1000
  286.1 3.6 %halve.12 = f32[1,1408,128]{2,1,0:T(8,128)} custom-call(s32[96]{0:T(128)} %dynamic-slice_bitcast_fusion.table_ref.core_ref, f32[8,704,128]{2,1,0:T(8,128)} %get-tuple-element.179.refs_0_, f32[8,704,128]{2,1,0:T(8,128)} %collective-permute-done.7.refs_1_, f32[4,704,128]{2,1,0:T(8,128)} %collective-permute-done.13.refs_2_, ...), custom_call_target="tpu_custom_call" | custom-call | bytes 300000 | tf_op jit(solution)/shard_map/halve/pallas_call | solution.py:986
  289.8 1.7 collective-permute-start.21
  291.5 3.8 %halve.13 = (f32[2,600,128]{2,1,0:T(8,128)}, f32[2,624,128]{2,1,0:T(8,128)}) custom-call(s32[96]{0:T(128)} %dynamic-slice_bitcast_fusion.table_ref.core_ref, f32[8,256,128]{2,1,0:T(8,128)} %get-tuple-element.182.refs_0_, f32[8,256,128]{2,1,0:T(8,128)} %collective-permute-done.10.refs_1_, f32[8,344,128]{2,1,0:T(8,128)} %get-tuple-element.178.refs_2_, ...), custom_call_target="tpu_custom_call" | custom-call | bytes 300000 | tf_op jit(solution)/shard_map/halve/pallas_call | solution.py:986
  297.2 4.2 %collective-permute-done.21 = f32[1408,128]{1,0:T(8,128)} collective-permute-done((f32[1408,128]{1,0:T(8,128)}, f32[1408,128]{1,0:T(8,128)}, u32[]{:S(2)}, u32[]{:S(2)}) %collective-permute-start.21) | collective-permute-done | bytes 720928 | tf_op jit(solution)/shard_map/ppermute | solution.py:1008
  301.4 2.3 bitcast_add_fusion
  304.1 1.8 collective-permute-done.26.refs_5_
  305.8 1.3 collective-permute-done.27.refs_11_.refs_12_
  307.2 3.2 halve.14
  310.5 3.9 %collective-permute-done.22 = f32[1408,128]{1,0:T(8,128)} collective-permute-done((f32[1408,128]{1,0:T(8,128)}, f32[1408,128]{1,0:T(8,128)}, u32[]{:S(2)}, u32[]{:S(2)}) %collective-permute-start.22) | collective-permute-done | bytes 720928 | tf_op jit(solution)/shard_map/ppermute | solution.py:1008
  314.4 2.3 add.21.a_ref
  316.9 3.5 halve.15
  321.5 8.5 %collective-permute-done.30 = f32[1224,128]{1,0:T(8,128)S(1)} collective-permute-done((f32[1224,128]{1,0:T(8,128)}, f32[1224,128]{1,0:T(8,128)S(1)}, u32[]{:S(2)}, u32[]{:S(2)}) %collective-permute-start.30) | collective-permute-done | bytes 626720 | tf_op jit(solution)/shard_map/ppermute | solution.py:1008
  330.0 1.1 slice_add_fusion.1
  331.2 1.9 collective-permute-start.31
  333.1 9.5 %collective-permute-done.31 = f32[1400,128]{1,0:T(8,128)S(1)} collective-permute-done((f32[1400,128]{1,0:T(8,128)S(1)}, f32[1400,128]{1,0:T(8,128)S(1)}, u32[]{:S(2)}, u32[]{:S(2)}) %collective-permute-start.31) | collective-permute-done | bytes 716832 | tf_op jit(solution)/shard_map/ppermute | solution.py:1008
  343.7 5.3 %collective-permute-start.32 = (f32[1752,128]{1,0:T(8,128)S(1)}, f32[1752,128]{1,0:T(8,128)}, u32[]{:S(2)}, u32[]{:S(2)}) collective-permute-start(f32[1752,128]{1,0:T(8,128)S(1)} %pad_maximum_fusion.b_ref), channel_id=1, source_target_pairs={{0,16},{16,0},{32,48},{48,32},{64,80},{80,64},{96,112},{112,96},{1... | collective-permute-start | bytes 2691080 | tf_op jit(solution)/shard_map/ppermute | solution.py:902
  349.0 3.0 collective-permute-done.23.a_other
  352.9 3.7 %unpack.1 = (f32[64,5632]{1,0:T(8,128)}, f32[176,1024]{1,0:T(8,128)}, f32[64,1024]{1,0:T(8,128)}, f32[64,3072]{1,0:T(8,128)}, f32[16,64]{1,0:T(8,128)}, /*index=...) custom-call(s32[96]{0:T(128)} %dynamic-slice_bitcast_fusion.table_ref.core_ref, ...), custom_call_target="tpu_custom_call" | custom-call | bytes 12000000 | tf_op jit(solution)/shard_map/unpack/pallas_call | solution.py:1058
  (53 shorter events, 8.9 us)
Async XLA Ops:
  14.1 25.4 %all-to-all-start = ((f32[16,136,128]{2,1,0:T(8,128)}), f32[16,136,128]{2,1,0:T(8,128)}, u32[]{:S(2)}, u32[]{:S(2)}) async-start(f32[16,136,128]{2,1,0:T(8,128)} %get-tuple-element.112), calls=%async_computation | async-start | bytes 2228224 | tf_op jit(solution)/shard_map/all_to_all | solution.py:898
  41.8 33.7 %collective-permute-start = (f32[1024,512]{1,0:T(8,128)}, f32[1024,512]{1,0:T(8,128)}, u32[]{:S(2)}, u32[]{:S(2)}) collective-permute-start(f32[1024,512]{1,0:T(8,128)} %get-tuple-element.127.refs_4_.refs_0_), channel_id=1, source_target_pairs={{0,16},{16,0},{32,48},{48,32},{64,80},{80,64},{96,112},{112,96},{1... | collective-permute-start | bytes 6291464 | tf_op jit(solution)/shard_map/ppermute | solution.py:902
  44.5 31.0 %collective-permute-start.1 = (f32[512,512]{1,0:T(8,128)}, f32[512,512]{1,0:T(8,128)}, u32[]{:S(2)}, u32[]{:S(2)}) collective-permute-start(f32[512,512]{1,0:T(8,128)} %get-tuple-element.129), channel_id=1, source_target_pairs={{0,16},{16,0},{32,48},{48,32},{64,80},{80,64},{96,112},{112,96},{1... | collective-permute-start | bytes 3145736 | tf_op jit(solution)/shard_map/ppermute | solution.py:902
  44.5 20.9 %all-to-all-start.1 = ((f32[16,128,128]{2,1,0:T(8,128)}), f32[16,128,128]{2,1,0:T(8,128)}, u32[]{:S(2)}, u32[]{:S(2)}) async-start(f32[16,128,128]{2,1,0:T(8,128)} %prefix.2), calls=%async_computation.1 | async-start | bytes 2097152 | tf_op jit(solution)/shard_map/all_to_all | solution.py:898
  102.3 23.2 %collective-permute-start.2 = (f32[2816,512]{1,0:T(8,128)}, f32[2816,512]{1,0:T(8,128)}, u32[]{:S(2)}, u32[]{:S(2)}) collective-permute-start(f32[2816,512]{1,0:T(8,128)} %get-tuple-element.138), channel_id=1, source_target_pairs={{0,16},{16,0},{32,48},{48,32},{64,80},{80,64},{96,112},{112,96},{1... | collective-permute-start | bytes 17301512 | tf_op jit(solution)/shard_map/ppermute | solution.py:902
  104.2 48.0 %collective-permute-start.5 = (f32[512,2816]{1,0:T(8,128)}, f32[512,2816]{1,0:T(8,128)}, u32[]{:S(2)}, u32[]{:S(2)}) collective-permute-start(f32[512,2816]{1,0:T(8,128)} %get-tuple-element.145), channel_id=1, source_target_pairs={{0,16},{16,0},{32,48},{48,32},{64,80},{80,64},{96,112},{112,96},{1... | collective-permute-start | bytes 17301512 | tf_op jit(solution)/shard_map/ppermute | solution.py:902
  104.5 47.8 %collective-permute-start.4 = (f32[2048,512]{1,0:T(8,128)}, f32[2048,512]{1,0:T(8,128)}, u32[]{:S(2)}, u32[]{:S(2)}) collective-permute-start(f32[2048,512]{1,0:T(8,128)} %get-tuple-element.143.mlpt_ref.refs_0_), channel_id=1, source_target_pairs={{0,16},{16,0},{32,48},{48,32},{64,80},{80,64},{96,112},{112,96},{1... | collective-permute-start | bytes 12582920 | tf_op jit(solution)/shard_map/ppermute | solution.py:902
  120.8 22.3 %all-to-all-start.2 = ((f32[16,128,128]{2,1,0:T(8,128)}), f32[16,128,128]{2,1,0:T(8,128)}, u32[]{:S(2)}, u32[]{:S(2)}) async-start(f32[16,128,128]{2,1,0:T(8,128)} %get-tuple-element.136), calls=%async_computation.2 | async-start | bytes 2097152 | tf_op jit(solution)/shard_map/all_to_all | solution.py:898
  125.1 27.1 %collective-permute-start.3 = (f32[512,1024]{1,0:T(8,128)}, f32[512,1024]{1,0:T(8,128)}, u32[]{:S(2)}, u32[]{:S(2)}) collective-permute-start(f32[512,1024]{1,0:T(8,128)} %get-tuple-element.142), channel_id=1, source_target_pairs={{0,16},{16,0},{32,48},{48,32},{64,80},{80,64},{96,112},{112,96},{1... | collective-permute-start | bytes 6291464 | tf_op jit(solution)/shard_map/ppermute | solution.py:902
  143.1 39.6 %collective-permute-start.6 = (f32[2,2816,128]{2,1,0:T(8,128)}, f32[2,2816,128]{2,1,0:T(8,128)}, u32[]{:S(2)}, u32[]{:S(2)}) collective-permute-start(f32[2,2816,128]{2,1,0:T(8,128)} %bitcast.46), channel_id=1, source_target_pairs={{0,32},{16,112},{32,0},{48,80},{64,96},{80,48},{96,64},{112,16},{1... | collective-permute-start | bytes 8650760 | tf_op jit(solution)/shard_map/ppermute | solution.py:1008
  147.9 23.2 %all-to-all-start.3 = ((f32[16,128,128]{2,1,0:T(8,128)}), f32[16,128,128]{2,1,0:T(8,128)}, u32[]{:S(2)}, u32[]{:S(2)}) async-start(f32[16,128,128]{2,1,0:T(8,128)} %prefix.3), calls=%async_computation.3 | async-start | bytes 2097152 | tf_op jit(solution)/shard_map/all_to_all | solution.py:898
  171.0 47.4 %collective-permute-start.7 = (f32[8,704,128]{2,1,0:T(8,128)}, f32[8,704,128]{2,1,0:T(8,128)}, u32[]{:S(2)}, u32[]{:S(2)}) collective-permute-start(f32[8,704,128]{2,1,0:T(8,128)} %get-tuple-element.168), channel_id=1, source_target_pairs={{0,4},{1,5},{2,6},{3,7},{4,0},{5,1},{6,2},{7,3},{8,12},{9,13},{10,... | collective-permute-start | bytes 8650760 | tf_op jit(solution)/shard_map/ppermute | solution.py:1000
  172.3 46.1 %collective-permute-start.8 = (f32[8,704,128]{2,1,0:T(8,128)}, f32[8,704,128]{2,1,0:T(8,128)}, u32[]{:S(2)}, u32[]{:S(2)}) collective-permute-start(f32[8,704,128]{2,1,0:T(8,128)} %get-tuple-element.171), channel_id=1, source_target_pairs={{0,1},{1,0},{2,3},{3,2},{4,5},{5,4},{6,7},{7,6},{8,9},{9,8},{10,11... | collective-permute-start | bytes 8650760 | tf_op jit(solution)/shard_map/ppermute | solution.py:1000
  186.0 32.4 %collective-permute-start.9 = (f32[1,2816,128]{2,1,0:T(8,128)}, f32[1,2816,128]{2,1,0:T(8,128)}, u32[]{:S(2)}, u32[]{:S(2)}) collective-permute-start(f32[1,2816,128]{2,1,0:T(8,128)} %halve_x.1), channel_id=1, source_target_pairs={{0,96},{16,48},{32,64},{48,16},{64,32},{80,112},{96,0},{112,80},{1... | collective-permute-start | bytes 4325384 | tf_op jit(solution)/shard_map/ppermute | solution.py:1008
  186.0 32.1 %collective-permute-start.10 = (f32[8,256,128]{2,1,0:T(8,128)}, f32[8,256,128]{2,1,0:T(8,128)}, u32[]{:S(2)}, u32[]{:S(2)}) collective-permute-start(f32[8,256,128]{2,1,0:T(8,128)} %get-tuple-element.175), channel_id=1, source_target_pairs={{0,4},{1,5},{2,6},{3,7},{4,0},{5,1},{6,2},{7,3},{8,12},{9,13},{10,... | collective-permute-start | bytes 3145736 | tf_op jit(solution)/shard_map/ppermute | solution.py:1000
  186.3 32.2 %collective-permute-start.11 = (f32[8,256,128]{2,1,0:T(8,128)}, f32[8,256,128]{2,1,0:T(8,128)}, u32[]{:S(2)}, u32[]{:S(2)}) collective-permute-start(f32[8,256,128]{2,1,0:T(8,128)} %get-tuple-element.176), channel_id=1, source_target_pairs={{0,1},{1,0},{2,3},{3,2},{4,5},{5,4},{6,7},{7,6},{8,9},{9,8},{10,11... | collective-permute-start | bytes 3145736 | tf_op jit(solution)/shard_map/ppermute | solution.py:1000
  218.4 6.0 %collective-permute-start.12 = (f32[512,1024]{1,0:T(8,128)}, f32[512,1024]{1,0:T(8,128)}, u32[]{:S(2)}, u32[]{:S(2)}) collective-permute-start(f32[512,1024]{1,0:T(8,128)} %get-tuple-element.177), channel_id=1, source_target_pairs={{0,16},{16,0},{32,48},{48,32},{64,80},{80,64},{96,112},{112,96},{1... | collective-permute-start | bytes 6291464 | tf_op jit(solution)/shard_map/ppermute | solution.py:902
  223.1 19.2 %collective-permute-start.13 = (f32[4,704,128]{2,1,0:T(8,128)}, f32[4,704,128]{2,1,0:T(8,128)}, u32[]{:S(2)}, u32[]{:S(2)}) collective-permute-start(f32[4,704,128]{2,1,0:T(8,128)} %get-tuple-element.172), channel_id=1, source_target_pairs={{0,12},{1,13},{2,14},{3,15},{4,8},{5,9},{6,10},{7,11},{8,4},{9,5},... | collective-permute-start | bytes 4325384 | tf_op jit(solution)/shard_map/ppermute | solution.py:1000
  224.4 20.4 %collective-permute-start.14 = (f32[4,704,128]{2,1,0:T(8,128)}, f32[4,704,128]{2,1,0:T(8,128)}, u32[]{:S(2)}, u32[]{:S(2)}) collective-permute-start(f32[4,704,128]{2,1,0:T(8,128)} %get-tuple-element.180), channel_id=1, source_target_pairs={{0,3},{1,2},{2,1},{3,0},{4,7},{5,6},{6,5},{7,4},{8,11},{9,10},{10,... | collective-permute-start | bytes 4325384 | tf_op jit(solution)/shard_map/ppermute | solution.py:1000
  234.3 26.9 %collective-permute-start.17 = (f32[8,368,128]{2,1,0:T(8,128)}, f32[8,368,128]{2,1,0:T(8,128)}, u32[]{:S(2)}, u32[]{:S(2)}) collective-permute-start(f32[8,368,128]{2,1,0:T(8,128)} %get-tuple-element.186), channel_id=1, source_target_pairs={{0,1},{1,0},{2,3},{3,2},{4,5},{5,4},{6,7},{7,6},{8,9},{9,8},{10,11... | collective-permute-start | bytes 4521992 | tf_op jit(solution)/shard_map/ppermute | solution.py:1000
  236.1 22.4 %collective-permute-start.16 = (f32[8,344,128]{2,1,0:T(8,128)}, f32[8,344,128]{2,1,0:T(8,128)}, u32[]{:S(2)}, u32[]{:S(2)}) collective-permute-start(f32[8,344,128]{2,1,0:T(8,128)} %get-tuple-element.183), channel_id=1, source_target_pairs={{0,4},{1,5},{2,6},{3,7},{4,0},{5,1},{6,2},{7,3},{8,12},{9,13},{10,... | collective-permute-start | bytes 4227080 | tf_op jit(solution)/shard_map/ppermute | solution.py:1000
  248.8 21.4 %collective-permute-start.15 = (f32[2,704,128]{2,1,0:T(8,128)}, f32[2,704,128]{2,1,0:T(8,128)}, u32[]{:S(2)}, u32[]{:S(2)}) collective-permute-start(f32[2,704,128]{2,1,0:T(8,128)} %get-tuple-element.181), channel_id=1, source_target_pairs={{0,1},{1,0},{2,3},{3,2},{4,5},{5,4},{6,7},{7,6},{8,9},{9,8},{10,11... | collective-permute-start | bytes 2162696 | tf_op jit(solution)/shard_map/ppermute | solution.py:1000
  250.6 19.5 %collective-permute-start.18 = (f32[2,704,128]{2,1,0:T(8,128)}, f32[2,704,128]{2,1,0:T(8,128)}, u32[]{:S(2)}, u32[]{:S(2)}) collective-permute-start(f32[2,704,128]{2,1,0:T(8,128)} %get-tuple-element.189), channel_id=1, source_target_pairs={{0,4},{1,5},{2,6},{3,7},{4,0},{5,1},{6,2},{7,3},{8,12},{9,13},{10,... | collective-permute-start | bytes 2162696 | tf_op jit(solution)/shard_map/ppermute | solution.py:1000
  265.5 25.9 %collective-permute-start.25 = (f32[4,624,128]{2,1,0:T(8,128)}, f32[4,624,128]{2,1,0:T(8,128)}, u32[]{:S(2)}, u32[]{:S(2)}) collective-permute-start(f32[4,624,128]{2,1,0:T(8,128)} %get-tuple-element.194), channel_id=1, source_target_pairs={{0,3},{1,2},{2,1},{3,0},{4,7},{5,6},{6,5},{7,4},{8,11},{9,10},{10,... | collective-permute-start | bytes 3833864 | tf_op jit(solution)/shard_map/ppermute | solution.py:1000
  265.6 25.9 %collective-permute-start.24 = (f32[4,600,128]{2,1,0:T(8,128)}, f32[4,600,128]{2,1,0:T(8,128)}, u32[]{:S(2)}, u32[]{:S(2)}) collective-permute-start(f32[4,600,128]{2,1,0:T(8,128)} %get-tuple-element.187), channel_id=1, source_target_pairs={{0,12},{1,13},{2,14},{3,15},{4,8},{5,9},{6,10},{7,11},{8,4},{9,5},... | collective-permute-start | bytes 3686408 | tf_op jit(solution)/shard_map/ppermute | solution.py:1000
  273.5 12.6 %collective-permute-start.19 = (f32[1,704,128]{2,1,0:T(8,128)}, f32[1,704,128]{2,1,0:T(8,128)}, u32[]{:S(2)}, u32[]{:S(2)}) collective-permute-start(f32[1,704,128]{2,1,0:T(8,128)} %get-tuple-element.190), channel_id=1, source_target_pairs={{0,3},{1,2},{2,1},{3,0},{4,7},{5,6},{6,5},{7,4},{8,11},{9,10},{10,... | collective-permute-start | bytes 1081352 | tf_op jit(solution)/shard_map/ppermute | solution.py:1000
  273.7 12.5 %collective-permute-start.20 = (f32[1,704,128]{2,1,0:T(8,128)}, f32[1,704,128]{2,1,0:T(8,128)}, u32[]{:S(2)}, u32[]{:S(2)}) collective-permute-start(f32[1,704,128]{2,1,0:T(8,128)} %get-tuple-element.191), channel_id=1, source_target_pairs={{0,12},{1,13},{2,14},{3,15},{4,8},{5,9},{6,10},{7,11},{8,4},{9,5},... | collective-permute-start | bytes 1081352 | tf_op jit(solution)/shard_map/ppermute | solution.py:1000
  289.8 11.7 %collective-permute-start.21 = (f32[1408,128]{1,0:T(8,128)}, f32[1408,128]{1,0:T(8,128)}, u32[]{:S(2)}, u32[]{:S(2)}) collective-permute-start(f32[1408,128]{1,0:T(8,128)} %bitcast.40), channel_id=1, source_target_pairs={{0,32},{16,112},{32,0},{48,80},{64,96},{80,48},{96,64},{112,16},{1... | collective-permute-start | bytes 2162696 | tf_op jit(solution)/shard_map/ppermute | solution.py:1008
  295.3 10.5 %collective-permute-start.26 = (f32[2,600,128]{2,1,0:T(8,128)}, f32[2,600,128]{2,1,0:T(8,128)}, u32[]{:S(2)}, u32[]{:S(2)}) collective-permute-start(f32[2,600,128]{2,1,0:T(8,128)} %get-tuple-element.195), channel_id=1, source_target_pairs={{0,1},{1,0},{2,3},{3,2},{4,5},{5,4},{6,7},{7,6},{8,9},{9,8},{10,11... | collective-permute-start | bytes 1843208 | tf_op jit(solution)/shard_map/ppermute | solution.py:1000
  296.4 10.8 %collective-permute-start.27 = (f32[2,624,128]{2,1,0:T(8,128)}, f32[2,624,128]{2,1,0:T(8,128)}, u32[]{:S(2)}, u32[]{:S(2)}) collective-permute-start(f32[2,624,128]{2,1,0:T(8,128)} %get-tuple-element.197), channel_id=1, source_target_pairs={{0,4},{1,5},{2,6},{3,7},{4,0},{5,1},{6,2},{7,3},{8,12},{9,13},{10,... | collective-permute-start | bytes 1916936 | tf_op jit(solution)/shard_map/ppermute | solution.py:1000
  303.7 10.7 %collective-permute-start.22 = (f32[1408,128]{1,0:T(8,128)}, f32[1408,128]{1,0:T(8,128)}, u32[]{:S(2)}, u32[]{:S(2)}) collective-permute-start(f32[1408,128]{1,0:T(8,128)} %bitcast_add_fusion), channel_id=1, source_target_pairs={{0,96},{16,48},{32,64},{48,16},{64,32},{80,112},{96,0},{112,80},{1... | collective-permute-start | bytes 2162696 | tf_op jit(solution)/shard_map/ppermute | solution.py:1008
  310.4 6.4 %collective-permute-start.29 = (f32[1,624,128]{2,1,0:T(8,128)}, f32[1,624,128]{2,1,0:T(8,128)}, u32[]{:S(2)}, u32[]{:S(2)}) collective-permute-start(f32[1,624,128]{2,1,0:T(8,128)} %get-tuple-element.199), channel_id=1, source_target_pairs={{0,12},{1,13},{2,14},{3,15},{4,8},{5,9},{6,10},{7,11},{8,4},{9,5},... | collective-permute-start | bytes 958472 | tf_op jit(solution)/shard_map/ppermute | solution.py:1000
  310.4 6.4 %collective-permute-start.28 = (f32[1,600,128]{2,1,0:T(8,128)}, f32[1,600,128]{2,1,0:T(8,128)}, u32[]{:S(2)}, u32[]{:S(2)}) collective-permute-start(f32[1,600,128]{2,1,0:T(8,128)} %get-tuple-element.198), channel_id=1, source_target_pairs={{0,3},{1,2},{2,1},{3,0},{4,7},{5,6},{6,5},{7,4},{8,11},{9,10},{10,... | collective-permute-start | bytes 921608 | tf_op jit(solution)/shard_map/ppermute | solution.py:1000
  320.4 9.6 %collective-permute-start.30 = (f32[1224,128]{1,0:T(8,128)}, f32[1224,128]{1,0:T(8,128)S(1)}, u32[]{:S(2)}, u32[]{:S(2)}) collective-permute-start(f32[1224,128]{1,0:T(8,128)} %bitcast.41), channel_id=1, source_target_pairs={{0,96},{16,48},{32,64},{48,16},{64,32},{80,112},{96,0},{112,80},{1... | collective-permute-start | bytes 1880072 | tf_op jit(solution)/shard_map/ppermute | solution.py:1008
  331.2 17.8 %copy-start.1 = (f32[1408,128]{1,0:T(8,128)S(1)}, f32[1408,128]{1,0:T(8,128)}, u32[]{:S(2)}) copy-start(f32[1408,128]{1,0:T(8,128)} %add.21.a_ref) | copy-start | bytes 2162692
  331.2 11.4 %collective-permute-start.31 = (f32[1400,128]{1,0:T(8,128)S(1)}, f32[1400,128]{1,0:T(8,128)S(1)}, u32[]{:S(2)}, u32[]{:S(2)}) collective-permute-start(f32[1400,128]{1,0:T(8,128)S(1)} %pad_maximum_fusion.1), channel_id=1, source_target_pairs={{0,32},{16,112},{32,0},{48,80},{64,96},{80,48},{96,64},{112,16},{1... | collective-permute-start | bytes 2150408 | tf_op jit(solution)/shard_map/ppermute | solution.py:1008
  342.7 1.0 copy-start
  343.7 9.2 %collective-permute-start.32 = (f32[1752,128]{1,0:T(8,128)S(1)}, f32[1752,128]{1,0:T(8,128)}, u32[]{:S(2)}, u32[]{:S(2)}) collective-permute-start(f32[1752,128]{1,0:T(8,128)S(1)} %pad_maximum_fusion.b_ref), channel_id=1, source_target_pairs={{0,16},{16,0},{32,48},{48,32},{64,80},{80,64},{96,112},{112,96},{1... | collective-permute-start | bytes 2691080 | tf_op jit(solution)/shard_map/ppermute | solution.py:902
  349.0 3.0 collective-permute-start.23
  352.0 0.9 copy-start.2
